TPU v7x, 32 devices: a whole 2x2x4 slice. The times are simulated.
32 devices in a mesh: layer: 2 (over x), row: 4 (over z), col: 4 (over y, core).
Axes of the slice: x: 2, y: 2, z: 4, core: 2. Of those that a mesh axis runs over, the one named last changes fastest.
Arguments:
- slab_tiles: bfloat16 [128, 16, 2, 4, 128], P(None, 'row', 'layer'), may hold values from -0.0546875 to 0.0546875
- x_tiles: bfloat16 [32, 4, 2, 128, 128], P(('layer', 'row', 'col')), may hold values from -6 to 6
- x_cols: int32 [32, 4, 2], P(('layer', 'row', 'col')), may hold values from 0 to 31, as said below
- x2_tiles: bfloat16 [32, 4, 2, 128, 128], P(('layer', 'row', 'col')), may hold values from -6 to 6
- x2_cols: int32 [32, 4, 2], P(('layer', 'row', 'col')), may hold values from 0 to 31, as said below
- requests: int32 [2, 4, 4], P('layer'), may hold values from 0 to 31, as said below
- out_cols: int32 [4, 4, 4], P('row', 'col'), may hold values from 0 to 31, as said below
Outputs:
- purified: bfloat16 [128, 16, 4, 4, 128], P('layer', 'row', 'col')
Inputs may be any that keep to these rules, and one draw needn't show every extreme that they name: Block row k is held by the device at index k of layer, row and col taken together. requests[l, r, q] is a block row held by layer l at row index (r + q * 1) % 4; every block row held by layer l is named exactly once in requests[l]. out_cols[r, c] holds 4 distinct block columns j, each with j % 4 == c. x_cols[k, c] holds 2 distinct block columns taken from out_cols[r, c], where r is the group whose requests name k. x2_cols[k, c] holds 2 distinct block columns taken from out_cols[r, c], where r is the group whose requests name k.
All inputs are finite; a program needn't handle non-finite values.
Results may differ from a plain program's by a relative error of at most 0.001.
Values may be sent and summed in bfloat16 or wider, within the bound.
No kernel may reach another device: no remote copies, remote signals or barrier semaphores. Data moves between devices by JAX's collectives and lax.ppermute only.
A program may use at most 64 MiB of HBM per device.

v0:
```python
import jax
import jax.numpy as jnp
from jax import lax
from jax.sharding import PartitionSpec as P


def as_sent(shard):
    return jax.tree.map(lambda a: a.astype(jnp.bfloat16) if a.dtype == jnp.float32 else a, shard)


def shifted(block, axis, distance):
    devices = range(lax.axis_size(axis))
    route = [((i - distance) % len(devices), i) for i in devices]
    return lax.ppermute(block, axis, route)


def choose_tiles(tile_set, col_ids, targets):
    matches = (col_ids[:, :, None] == targets[None, None, :]).astype(jnp.bfloat16)
    chosen = jnp.einsum("qus,qubd->qbsd", matches, tile_set, preferred_element_type=jnp.float32)
    return chosen.astype(jnp.bfloat16).reshape(
        tile_set.shape[0] * tile_set.shape[2], targets.shape[0] * tile_set.shape[3]
    )


def body(slab_tiles, x_tiles, x_cols, x2_tiles, x2_cols, requests, out_cols):
    grid_rows = lax.axis_size("row")
    col_groups = lax.axis_size("col")
    stride = grid_rows // col_groups
    arrived = (
        lax.all_to_all(x_tiles, "col", split_axis=1, concat_axis=0, tiled=True),
        lax.all_to_all(x_cols, "col", split_axis=1, concat_axis=0, tiled=True),
        lax.all_to_all(x2_tiles, "col", split_axis=1, concat_axis=0, tiled=True),
        lax.all_to_all(x2_cols, "col", split_axis=1, concat_axis=0, tiled=True),
    )
    held_first, first_ids, held_second, second_ids = arrived
    own_row = lax.axis_index("row")
    wanted = requests[0]

    def pick_held(values, owner):
        return lax.dynamic_index_in_dim(values, owner, 0, keepdims=False)[0]

    got_first, got_first_ids, got_second, got_second_ids = ([], [], [], [])
    for slot in range(col_groups):
        offset = slot * stride
        reader = (own_row - offset + grid_rows) % grid_rows
        owner = lax.dynamic_index_in_dim(wanted[:, slot], reader, 0, keepdims=False) % col_groups
        sent = (
            pick_held(held_first, owner),
            pick_held(first_ids, owner),
            pick_held(held_second, owner),
            pick_held(second_ids, owner),
        )
        back = shifted(
            (sent[0], as_sent(sent[1]), sent[2], as_sent(sent[3])),
            "row",
            (grid_rows - offset) % grid_rows,
        )
        got_first.append(back[0])
        got_first_ids.append(back[1])
        got_second.append(back[2])
        got_second_ids.append(back[3])
    targets = out_cols[0, 0]
    chosen_first = choose_tiles(jnp.stack(got_first), jnp.stack(got_first_ids), targets)
    chosen_second = choose_tiles(jnp.stack(got_second), jnp.stack(got_second_ids), targets)
    layer_rows = slab_tiles.shape[0] // lax.axis_size("layer")
    left_rows = slab_tiles.reshape(
        lax.axis_size("layer") * layer_rows * slab_tiles.shape[1],
        slab_tiles.shape[3] * slab_tiles.shape[4],
    )
    first_term = jnp.dot(left_rows, chosen_first, preferred_element_type=jnp.float32)
    second_term = jnp.dot(left_rows, chosen_second, preferred_element_type=jnp.float32)
    summed = lax.psum_scatter(
        (4.0 * first_term - 3.0 * second_term).reshape(
            (
                lax.axis_size("layer") * layer_rows,
                slab_tiles.shape[1],
                1,
                targets.shape[0],
                slab_tiles.shape[4],
            )
        ),
        "layer",
        scatter_dimension=0,
        tiled=True,
    )
    return summed.astype(jnp.bfloat16)


def solution(mesh):
    placed = (
        P(None, "row", "layer", None, None),
        P(("layer", "row", "col"), None, None, None, None),
        P(("layer", "row", "col"), None, None),
        P(("layer", "row", "col"), None, None, None, None),
        P(("layer", "row", "col"), None, None),
        P("layer", None, None),
        P("row", "col", None),
    )
    return jax.shard_map(
        body,
        mesh=mesh,
        in_specs=placed,
        out_specs=P("layer", "row", "col", None, None),
        check_vma=False,
    )
```

profile of v0, /device:TPU:0, one launch (start us, length us, event | category | flops | bytes accessed | tf_op | source)
XLA Modules:
  0.0 92.8 jit_solution(7264105289062823389)
XLA Ops:
  6.5 1.3 %copy.32 = s32[1,4,2]{2,0,1:T(1,128)} copy(s32[1,4,2]{1,2,0:T(2,128)} %param.9) | data formatting | bytes 64 | tf_op args[2]
  7.9 4.2 %all-to-all-start.1 = ((s32[1,4,2]{2,0,1:T(1,128)}), s32[1,4,2]{2,0,1:T(1,128)S(1)}, u32[]{:S(2)}, u32[]{:S(2)}) async-start(s32[1,4,2]{2,0,1:T(1,128)} %copy.32), calls=%async_computation.1 | async-start | bytes 4096 | tf_op jit(solution)/shard_map/all_to_all | solution.py:31
  12.1 0.7 copy-done.1
  12.8 0.1 fusion.43
  12.9 0.6 constant_dynamic-slice_fusion.17
  17.2 0.6 constant_dynamic-slice_fusion.13
  21.5 0.0 copy-start.2
  21.5 0.7 copy-done.2
  22.2 0.7 copy.38
  22.9 0.0 all-to-all-done.1
  22.9 3.3 %all-to-all-start.3 = ((s32[1,4,2]{2,0,1:T(1,128)}), s32[1,4,2]{2,0,1:T(1,128)S(1)}, u32[]{:S(2)}, u32[]{:S(2)}) async-start(s32[1,4,2]{2,0,1:T(1,128)} %copy.38), calls=%async_computation.3 | async-start | bytes 4096 | tf_op jit(solution)/shard_map/all_to_all | solution.py:33
  26.2 0.0 collective-permute-start.4
  26.2 2.0 %collective-permute-start.7 = (s32[2]{0:T(128)S(1)}, s32[2]{0:T(128)S(1)}, u32[]{:S(2)}, u32[]{:S(2)}) collective-permute-start(s32[2]{0:T(128)S(1)} %get-tuple-element.18), channel_id=1, source_target_pairs={{12,0},{0,4},{4,8},{8,12},{13,1},{1,5},{5,9},{9,13},{14,2},{2,6},{... | collective-permute-start | bytes 32 | tf_op jit(solution)/shard_map/ppermute | solution.py:14
  28.2 2.6 %collective-permute-start.6 = (s32[2]{0:T(128)S(1)}, s32[2]{0:T(128)S(1)}, u32[]{:S(2)}, u32[]{:S(2)}) collective-permute-start(s32[2]{0:T(128)S(1)} %get-tuple-element.19), channel_id=1, source_target_pairs={{8,0},{12,4},{0,8},{4,12},{9,1},{13,5},{1,9},{5,13},{10,2},{14,6},... | collective-permute-start | bytes 32 | tf_op jit(solution)/shard_map/ppermute | solution.py:14
  30.8 1.3 %collective-permute-start.5 = (s32[2]{0:T(128)S(1)}, s32[2]{0:T(128)S(1)}, u32[]{:S(2)}, u32[]{:S(2)}) collective-permute-start(s32[2]{0:T(128)S(1)} %get-tuple-element.20), channel_id=1, source_target_pairs={{4,0},{8,4},{12,8},{0,12},{5,1},{9,5},{13,9},{1,13},{6,2},{10,6},{... | collective-permute-start | bytes 32 | tf_op jit(solution)/shard_map/ppermute | solution.py:14
  32.1 0.0 all-to-all-done.3
  32.1 3.4 %all-to-all-start = ((bf16[1,4,2,128,128]{4,3,2,0,1:T(8,128)(2,1)}), bf16[1,4,2,128,128]{4,3,2,0,1:T(8,128)(2,1)S(1)}, u32[]{:S(2)}, u32[]{:S(2)}) async-start(bf16[1,4,2,128,128]{4,3,2,0,1:T(8,128)(2,1)} %bitcast), calls=%async_computation | async-start | bytes 524288 | tf_op jit(solution)/shard_map/all_to_all | solution.py:30
  35.6 0.7 collective-permute-start.15
  36.3 0.0 collective-permute-done.7
  36.3 1.7 %collective-permute-start.14 = (s32[2]{0:T(128)S(1)}, s32[2]{0:T(128)S(1)}, u32[]{:S(2)}, u32[]{:S(2)}) collective-permute-start(s32[2]{0:T(128)S(1)} %get-tuple-element.15), channel_id=1, source_target_pairs={{8,0},{12,4},{0,8},{4,12},{9,1},{13,5},{1,9},{5,13},{10,2},{14,6},... | collective-permute-start | bytes 32 | tf_op jit(solution)/shard_map/ppermute | solution.py:14
  38.0 0.0 collective-permute-done.6
  38.0 1.5 %collective-permute-start.13 = (s32[2]{0:T(128)S(1)}, s32[2]{0:T(128)S(1)}, u32[]{:S(2)}, u32[]{:S(2)}) collective-permute-start(s32[2]{0:T(128)S(1)} %get-tuple-element.16), channel_id=1, source_target_pairs={{4,0},{8,4},{12,8},{0,12},{5,1},{9,5},{13,9},{1,13},{6,2},{10,6},{... | collective-permute-start | bytes 32 | tf_op jit(solution)/shard_map/ppermute | solution.py:14
  39.5 0.0 collective-permute-done.5
  39.6 2.0 %all-to-all-done = bf16[1,4,2,128,128]{4,3,2,0,1:T(8,128)(2,1)S(1)} async-done(((bf16[1,4,2,128,128]{4,3,2,0,1:T(8,128)(2,1)}), bf16[1,4,2,128,128]{4,3,2,0,1:T(8,128)(2,1)S(1)}, u32[]{:S(2)}, u32[]{:S(2)}) %all-to-all-start) | async-done | bytes 262176 | tf_op jit(solution)/shard_map/all_to_all | solution.py:30
  41.6 3.4 %all-to-all-start.2 = ((bf16[1,4,2,128,128]{4,3,2,0,1:T(8,128)(2,1)}), bf16[1,4,2,128,128]{4,3,2,0,1:T(8,128)(2,1)S(1)}, u32[]{:S(2)}, u32[]{:S(2)}) async-start(bf16[1,4,2,128,128]{4,3,2,0,1:T(8,128)(2,1)} %bitcast.26), calls=%async_computation.2 | async-start | bytes 524288 | tf_op jit(solution)/shard_map/all_to_all | solution.py:32
  45.0 0.0 reduce-scatter.5.cloned.1.call-start
  45.0 0.0 collective-permute-done.12
  45.0 0.0 collective-permute-done.15
  45.0 0.0 collective-permute-done.13
  45.1 0.1 copy.79
  45.2 0.1 copy.76
  45.3 0.1 copy.77
  45.3 0.1 copy.78
  45.4 1.8 %collective-permute-start.1 = (bf16[2,128,128]{2,0,1:T(2,128)(2,1)S(1)}, bf16[2,128,128]{2,0,1:T(2,128)(2,1)S(1)}, u32[]{:S(2)}, u32[]{:S(2)}) collective-permute-start(bf16[2,128,128]{2,0,1:T(2,128)(2,1)S(1)} %bitcast.119), channel_id=1, source_target_pairs={{4,0},{8,4},{12,8},{0,12},{5,1},{9,5},{13,9},{1,13},{6,2},{10,6},{... | collective-permute-start | bytes 196616 | tf_op jit(solution)/shard_map/ppermute | solution.py:14
  47.2 0.4 collective-permute-start.2
  47.6 0.6 collective-permute-start.3
  48.3 0.0 collective-permute-start
  48.3 2.7 %all-to-all-done.2 = bf16[1,4,2,128,128]{4,3,2,0,1:T(8,128)(2,1)S(1)} async-done(((bf16[1,4,2,128,128]{4,3,2,0,1:T(8,128)(2,1)}), bf16[1,4,2,128,128]{4,3,2,0,1:T(8,128)(2,1)S(1)}, u32[]{:S(2)}, u32[]{:S(2)}) %all-to-all-start.2) | async-done | bytes 262176 | tf_op jit(solution)/shard_map/all_to_all | solution.py:32
  51.0 0.1 copy.75
  51.1 0.1 copy.72
  51.1 0.1 copy.73
  51.2 0.1 copy.74
  51.3 1.8 %collective-permute-start.9 = (bf16[2,128,128]{2,0,1:T(2,128)(2,1)S(1)}, bf16[2,128,128]{2,0,1:T(2,128)(2,1)S(1)}, u32[]{:S(2)}, u32[]{:S(2)}) collective-permute-start(bf16[2,128,128]{2,0,1:T(2,128)(2,1)S(1)} %bitcast.120), channel_id=1, source_target_pairs={{4,0},{8,4},{12,8},{0,12},{5,1},{9,5},{13,9},{1,13},{6,2},{10,6},{... | collective-permute-start | bytes 196616 | tf_op jit(solution)/shard_map/ppermute | solution.py:14
  53.1 0.4 collective-permute-start.10
  53.5 1.4 %collective-permute-done.2 = bf16[2,128,128]{2,0,1:T(2,128)(2,1)S(1)} collective-permute-done((bf16[2,128,128]{2,0,1:T(2,128)(2,1)S(1)}, bf16[2,128,128]{2,0,1:T(2,128)(2,1)S(1)}, u32[]{:S(2)}, u32[]{:S(2)}) %collective-permute-start.2) | collective-permute-done | bytes 65568 | tf_op jit(solution)/shard_map/ppermute | solution.py:14
  54.9 0.0 collective-permute-start.8
  54.9 0.0 copy-start.3
  54.9 0.6 copy-done.3
  55.6 0.5 convolution_convert_fusion.1
  56.2 0.5 copy-done
  56.6 0.5 convolution_multiply_fusion.1
  57.1 0.0 collective-permute-done.9
  57.1 1.9 %collective-permute-done.10 = bf16[2,128,128]{2,0,1:T(2,128)(2,1)S(1)} collective-permute-done((bf16[2,128,128]{2,0,1:T(2,128)(2,1)S(1)}, bf16[2,128,128]{2,0,1:T(2,128)(2,1)S(1)}, u32[]{:S(2)}, u32[]{:S(2)}) %collective-permute-start.10) | collective-permute-done | bytes 65568 | tf_op jit(solution)/shard_map/ppermute | solution.py:14
  59.0 2.0 %collective-permute-done.11 = bf16[2,128,128]{2,0,1:T(2,128)(2,1)S(1)} collective-permute-done((bf16[2,128,128]{2,0,1:T(2,128)(2,1)S(1)}, bf16[2,128,128]{2,0,1:T(2,128)(2,1)S(1)}, u32[]{:S(2)}, u32[]{:S(2)}) %collective-permute-start.11) | collective-permute-done | bytes 65568 | tf_op jit(solution)/shard_map/ppermute | solution.py:14
  61.0 0.0 collective-permute-done.8
  61.0 0.5 convolution_convert_fusion
  61.5 0.5 fusion.1
  62.0 0.3 copy.39
  62.4 0.4 reshape.93
  62.7 1.4 %reshape.96 = f32[128,2048]{1,0:T(8,128)} reshape(f32[128,1,4,4,128]{4,3,2,1,0:T(4,128)S(1)} %bitcast.109) | data formatting | bytes 2097152
  64.1 0.0 reduce-scatter.5.cloned.1.call-update
  64.2 19.8 %reduce-scatter.5.cloned.1.call-done = f32[64,2048]{1,0:T(8,128)} async-done(((f32[128,2048]{1,0:T(8,128)}), f32[64,2048]{1,0:T(8,128)}) %reduce-scatter.5.cloned.1.call-update) | async-done | bytes 524304
  84.0 1.1 %reshape.97 = bf16[64,1,4,4,128]{4,3,2,1,0:T(4,128)(2,1)S(1)} reshape(f32[64,2048]{1,0:T(8,128)} %reduce-scatter.5.cloned.1.call-done) | data formatting | bytes 786432
  85.1 0.8 fusion.10
  (15 shorter events, 0.1 us)
Async XLA Ops:
  7.9 15.0 %all-to-all-start.1 = ((s32[1,4,2]{2,0,1:T(1,128)}), s32[1,4,2]{2,0,1:T(1,128)S(1)}, u32[]{:S(2)}, u32[]{:S(2)}) async-start(s32[1,4,2]{2,0,1:T(1,128)} %copy.32), calls=%async_computation.1 | async-start | bytes 4096 | tf_op jit(solution)/shard_map/all_to_all | solution.py:31
  12.1 0.7 copy-start.1
  21.5 0.7 copy-start.2
  22.9 9.3 %all-to-all-start.3 = ((s32[1,4,2]{2,0,1:T(1,128)}), s32[1,4,2]{2,0,1:T(1,128)S(1)}, u32[]{:S(2)}, u32[]{:S(2)}) async-start(s32[1,4,2]{2,0,1:T(1,128)} %copy.38), calls=%async_computation.3 | async-start | bytes 4096 | tf_op jit(solution)/shard_map/all_to_all | solution.py:33
  26.2 9.4 %collective-permute-start.4 = (s32[2]{0:T(128)S(1)}, s32[2]{0:T(128)S(1)}, u32[]{:S(2)}, u32[]{:S(2)}) collective-permute-start(s32[2]{0:T(128)S(1)} %get-tuple-element.17), channel_id=1, source_target_pairs={{0,0},{4,4},{8,8},{12,12},{1,1},{5,5},{9,9},{13,13},{2,2},{6,6},{1... | collective-permute-start | bytes 32 | tf_op jit(solution)/shard_map/ppermute | solution.py:14
  26.2 10.2 %collective-permute-start.7 = (s32[2]{0:T(128)S(1)}, s32[2]{0:T(128)S(1)}, u32[]{:S(2)}, u32[]{:S(2)}) collective-permute-start(s32[2]{0:T(128)S(1)} %get-tuple-element.18), channel_id=1, source_target_pairs={{12,0},{0,4},{4,8},{8,12},{13,1},{1,5},{5,9},{9,13},{14,2},{2,6},{... | collective-permute-start | bytes 32 | tf_op jit(solution)/shard_map/ppermute | solution.py:14
  28.2 9.8 %collective-permute-start.6 = (s32[2]{0:T(128)S(1)}, s32[2]{0:T(128)S(1)}, u32[]{:S(2)}, u32[]{:S(2)}) collective-permute-start(s32[2]{0:T(128)S(1)} %get-tuple-element.19), channel_id=1, source_target_pairs={{8,0},{12,4},{0,8},{4,12},{9,1},{13,5},{1,9},{5,13},{10,2},{14,6},... | collective-permute-start | bytes 32 | tf_op jit(solution)/shard_map/ppermute | solution.py:14
  30.8 8.8 %collective-permute-start.5 = (s32[2]{0:T(128)S(1)}, s32[2]{0:T(128)S(1)}, u32[]{:S(2)}, u32[]{:S(2)}) collective-permute-start(s32[2]{0:T(128)S(1)} %get-tuple-element.20), channel_id=1, source_target_pairs={{4,0},{8,4},{12,8},{0,12},{5,1},{9,5},{13,9},{1,13},{6,2},{10,6},{... | collective-permute-start | bytes 32 | tf_op jit(solution)/shard_map/ppermute | solution.py:14
  32.1 9.4 %all-to-all-start = ((bf16[1,4,2,128,128]{4,3,2,0,1:T(8,128)(2,1)}), bf16[1,4,2,128,128]{4,3,2,0,1:T(8,128)(2,1)S(1)}, u32[]{:S(2)}, u32[]{:S(2)}) async-start(bf16[1,4,2,128,128]{4,3,2,0,1:T(8,128)(2,1)} %bitcast), calls=%async_computation | async-start | bytes 524288 | tf_op jit(solution)/shard_map/all_to_all | solution.py:30
  35.6 9.4 %collective-permute-start.12 = (s32[2]{0:T(128)S(1)}, s32[2]{0:T(128)S(1)}, u32[]{:S(2)}, u32[]{:S(2)}) collective-permute-start(s32[2]{0:T(128)S(1)} %get-tuple-element.13), channel_id=1, source_target_pairs={{0,0},{4,4},{8,8},{12,12},{1,1},{5,5},{9,9},{13,13},{2,2},{6,6},{1... | collective-permute-start | bytes 32 | tf_op jit(solution)/shard_map/ppermute | solution.py:14
  35.6 9.4 %collective-permute-start.15 = (s32[2]{0:T(128)S(1)}, s32[2]{0:T(128)S(1)}, u32[]{:S(2)}, u32[]{:S(2)}) collective-permute-start(s32[2]{0:T(128)S(1)} %get-tuple-element.14), channel_id=1, source_target_pairs={{12,0},{0,4},{4,8},{8,12},{13,1},{1,5},{5,9},{9,13},{14,2},{2,6},{... | collective-permute-start | bytes 32 | tf_op jit(solution)/shard_map/ppermute | solution.py:14
  36.3 8.7 %collective-permute-start.14 = (s32[2]{0:T(128)S(1)}, s32[2]{0:T(128)S(1)}, u32[]{:S(2)}, u32[]{:S(2)}) collective-permute-start(s32[2]{0:T(128)S(1)} %get-tuple-element.15), channel_id=1, source_target_pairs={{8,0},{12,4},{0,8},{4,12},{9,1},{13,5},{1,9},{5,13},{10,2},{14,6},... | collective-permute-start | bytes 32 | tf_op jit(solution)/shard_map/ppermute | solution.py:14
  38.0 7.1 %collective-permute-start.13 = (s32[2]{0:T(128)S(1)}, s32[2]{0:T(128)S(1)}, u32[]{:S(2)}, u32[]{:S(2)}) collective-permute-start(s32[2]{0:T(128)S(1)} %get-tuple-element.16), channel_id=1, source_target_pairs={{4,0},{8,4},{12,8},{0,12},{5,1},{9,5},{13,9},{1,13},{6,2},{10,6},{... | collective-permute-start | bytes 32 | tf_op jit(solution)/shard_map/ppermute | solution.py:14
  41.6 9.4 %all-to-all-start.2 = ((bf16[1,4,2,128,128]{4,3,2,0,1:T(8,128)(2,1)}), bf16[1,4,2,128,128]{4,3,2,0,1:T(8,128)(2,1)S(1)}, u32[]{:S(2)}, u32[]{:S(2)}) async-start(bf16[1,4,2,128,128]{4,3,2,0,1:T(8,128)(2,1)} %bitcast.26), calls=%async_computation.2 | async-start | bytes 524288 | tf_op jit(solution)/shard_map/all_to_all | solution.py:32
  45.0 39.0 %reduce-scatter.5.cloned.1.call-start = ((), (), s32[]{:S(2)}) async-start(), calls=%async_computation.5 | async-start | bytes 1572864
  45.4 7.7 %collective-permute-start.1 = (bf16[2,128,128]{2,0,1:T(2,128)(2,1)S(1)}, bf16[2,128,128]{2,0,1:T(2,128)(2,1)S(1)}, u32[]{:S(2)}, u32[]{:S(2)}) collective-permute-start(bf16[2,128,128]{2,0,1:T(2,128)(2,1)S(1)} %bitcast.119), channel_id=1, source_target_pairs={{4,0},{8,4},{12,8},{0,12},{5,1},{9,5},{13,9},{1,13},{6,2},{10,6},{... | collective-permute-start | bytes 196616 | tf_op jit(solution)/shard_map/ppermute | solution.py:14
  47.2 7.7 %collective-permute-start.2 = (bf16[2,128,128]{2,0,1:T(2,128)(2,1)S(1)}, bf16[2,128,128]{2,0,1:T(2,128)(2,1)S(1)}, u32[]{:S(2)}, u32[]{:S(2)}) collective-permute-start(bf16[2,128,128]{2,0,1:T(2,128)(2,1)S(1)} %bitcast.116), channel_id=1, source_target_pairs={{8,0},{12,4},{0,8},{4,12},{9,1},{13,5},{1,9},{5,13},{10,2},{14,6},... | collective-permute-start | bytes 196616 | tf_op jit(solution)/shard_map/ppermute | solution.py:14
  47.6 7.3 %collective-permute-start.3 = (bf16[2,128,128]{2,0,1:T(2,128)(2,1)S(1)}, bf16[2,128,128]{2,0,1:T(2,128)(2,1)S(1)}, u32[]{:S(2)}, u32[]{:S(2)}) collective-permute-start(bf16[2,128,128]{2,0,1:T(2,128)(2,1)S(1)} %bitcast.114), channel_id=1, source_target_pairs={{12,0},{0,4},{4,8},{8,12},{13,1},{1,5},{5,9},{9,13},{14,2},{2,6},{... | collective-permute-start | bytes 196616 | tf_op jit(solution)/shard_map/ppermute | solution.py:14
  48.3 6.7 %collective-permute-start = (bf16[2,128,128]{2,0,1:T(2,128)(2,1)S(1)}, bf16[2,128,128]{2,0,1:T(2,128)(2,1)S(1)}, u32[]{:S(2)}, u32[]{:S(2)}) collective-permute-start(bf16[2,128,128]{2,0,1:T(2,128)(2,1)S(1)} %bitcast.113), channel_id=1, source_target_pairs={{0,0},{4,4},{8,8},{12,12},{1,1},{5,5},{9,9},{13,13},{2,2},{6,6},{1... | collective-permute-start | bytes 196616 | tf_op jit(solution)/shard_map/ppermute | solution.py:14
  51.3 5.8 %collective-permute-start.9 = (bf16[2,128,128]{2,0,1:T(2,128)(2,1)S(1)}, bf16[2,128,128]{2,0,1:T(2,128)(2,1)S(1)}, u32[]{:S(2)}, u32[]{:S(2)}) collective-permute-start(bf16[2,128,128]{2,0,1:T(2,128)(2,1)S(1)} %bitcast.120), channel_id=1, source_target_pairs={{4,0},{8,4},{12,8},{0,12},{5,1},{9,5},{13,9},{1,13},{6,2},{10,6},{... | collective-permute-start | bytes 196616 | tf_op jit(solution)/shard_map/ppermute | solution.py:14
  53.1 5.9 %collective-permute-start.10 = (bf16[2,128,128]{2,0,1:T(2,128)(2,1)S(1)}, bf16[2,128,128]{2,0,1:T(2,128)(2,1)S(1)}, u32[]{:S(2)}, u32[]{:S(2)}) collective-permute-start(bf16[2,128,128]{2,0,1:T(2,128)(2,1)S(1)} %bitcast.118), channel_id=1, source_target_pairs={{8,0},{12,4},{0,8},{4,12},{9,1},{13,5},{1,9},{5,13},{10,2},{14,6},... | collective-permute-start | bytes 196616 | tf_op jit(solution)/shard_map/ppermute | solution.py:14
  54.9 6.1 %collective-permute-start.11 = (bf16[2,128,128]{2,0,1:T(2,128)(2,1)S(1)}, bf16[2,128,128]{2,0,1:T(2,128)(2,1)S(1)}, u32[]{:S(2)}, u32[]{:S(2)}) collective-permute-start(bf16[2,128,128]{2,0,1:T(2,128)(2,1)S(1)} %bitcast.117), channel_id=1, source_target_pairs={{12,0},{0,4},{4,8},{8,12},{13,1},{1,5},{5,9},{9,13},{14,2},{2,6},{... | collective-permute-start | bytes 196616 | tf_op jit(solution)/shard_map/ppermute | solution.py:14
  54.9 6.1 %collective-permute-start.8 = (bf16[2,128,128]{2,0,1:T(2,128)(2,1)S(1)}, bf16[2,128,128]{2,0,1:T(2,128)(2,1)S(1)}, u32[]{:S(2)}, u32[]{:S(2)}) collective-permute-start(bf16[2,128,128]{2,0,1:T(2,128)(2,1)S(1)} %bitcast.115), channel_id=1, source_target_pairs={{0,0},{4,4},{8,8},{12,12},{1,1},{5,5},{9,9},{13,13},{2,2},{6,6},{1... | collective-permute-start | bytes 196616 | tf_op jit(solution)/shard_map/ppermute | solution.py:14
  54.9 0.7 copy-start.3
  55.6 1.0 %copy-start = (bf16[128,4,1,4,128]{4,3,2,1,0:T(4,128)(2,1)S(1)}, bf16[128,4,1,4,128]{4,3,2,1,0:T(4,128)(2,1)}, u32[]{:S(2)}) copy-start(bf16[128,4,1,4,128]{4,3,2,1,0:T(4,128)(2,1)} %param.7) | copy-start | bytes 1572868
Sparse Core Ops, SparseCore 0:
  64.3 19.6 reduce-scatter.4
where the time goes:
time: 93.4 us; the launch traced here: 92.8 us
  waiting for transfers between devices  29.8 us (32%)
  starting transfers between devices  29.3 us (31%)
  between operations  21.1 us (23%)
  local copies, waits for them, and re-layouts  10.4 us (11%)
  matrix products  2.07 us (2%)
    unnamed x2, waiting for transfers between devices  19.8 us
    ppermute x16, starting transfers between devices, shifted(): return lax.ppermute(block, axis, route)  15 us
    unnamed x12, local copies, waits for them, and re-layouts  7.04 us
    ppermute x16, waiting for transfers between devices, shifted(): return lax.ppermute(block, axis, route)  5.27 us
    all_to_all x1, starting transfers between devices, body(): lax.all_to_all(x_cols, 'col', split_axis=1, concat_axis=0, tiled=True)  4.24 us
    all_to_all x1, starting transfers between devices, body(): lax.all_to_all(x_tiles, 'col', split_axis=1, concat_axis=0, tiled=True)  3.41 us
    all_to_all x1, starting transfers between devices, body(): lax.all_to_all(x2_tiles, 'col', split_axis=1, concat_axis=0, tiled=True)  3.41 us
    all_to_all x1, starting transfers between devices, body(): lax.all_to_all(x2_cols, 'col', split_axis=1, concat_axis=0, tiled=True)  3.29 us
  transfers between devices with their start and end apart: 21, of which 6 were waited for; matrix products, arithmetic and copies ran while one was open for 4% of the time, Pallas kernels for 0%

commit v1 on v0

v1 whole, which is shorter than its diff:
```python
import functools

import jax
import jax.numpy as jnp
from jax import lax
from jax.experimental import pallas as pl
from jax.experimental.pallas import tpu as pltpu
from jax.sharding import PartitionSpec as P

DIGIT = 8
VMEM = pl.BlockSpec(memory_space=pltpu.VMEM)
SMEM = pl.BlockSpec(memory_space=pltpu.SMEM)


def mate(index, step, size):
    return index ^ step if size & (size - 1) == 0 else (index - step) % size


def target(index, step, size):
    return index ^ step if size & (size - 1) == 0 else (index + step) % size


def round_of(index, source, size):
    return index ^ source if size & (size - 1) == 0 else lax.rem(index - source + size, size)


def exchange(block, axis, step, size, stride=1):
    route = []
    for place in range(size * stride):
        high, low = divmod(place, stride)
        route.append((place, target(high, step, size) * stride + low))
    return lax.ppermute(block, axis, route)


def id_rows(stored):
    return -(-4 * stored // 16) * 16


def pack_kernel(x_ref, x2_ref, cols_ref, cols2_ref, *outs):
    groups, stored, side = x_ref.shape[1:4]
    own = lax.axis_index("col")
    count = id_rows(stored)
    row = lax.broadcasted_iota(jnp.int32, (count, side), 0)
    for step, out in enumerate(outs):
        reader = target(own, step, groups)
        digits = jnp.zeros((count, side), jnp.int32)
        for part, (ref, cols) in enumerate(((x_ref, cols_ref), (x2_ref, cols2_ref))):
            for at in range(stored):
                place = part * stored + at
                out[pl.ds(place * side, side), :] = ref[0, reader, at]
                value = cols[0, at, reader]
                digits = jnp.where(row == 2 * place, value >> DIGIT, digits)
                digits = jnp.where(row == 2 * place + 1, value & ((1 << DIGIT) - 1), digits)
        out[pl.ds(2 * stored * side, count), :] = digits.astype(jnp.float32).astype(out.dtype)


def pack(x_tiles, x2_tiles, x_cols, x2_cols):
    _, groups, stored, side, _ = x_tiles.shape
    shape = jax.ShapeDtypeStruct((2 * stored * side + id_rows(stored), side), x_tiles.dtype)
    return pl.pallas_call(
        pack_kernel,
        out_shape=[shape] * groups,
        in_specs=[VMEM, VMEM, SMEM, SMEM],
        out_specs=[VMEM] * groups,
        name="pack",
    )(x_tiles, x2_tiles, jnp.swapaxes(x_cols, 1, 2), jnp.swapaxes(x2_cols, 1, 2))


def pick_kernel(stride, wanted_ref, *rest):
    groups = len(rest) // 2
    held, outs = rest[:groups], rest[groups:]
    own_row, own_col = lax.axis_index("row"), lax.axis_index("col")
    high, low = own_row // stride, own_row % stride
    for step, out in enumerate(outs):
        reader = target(high, step, groups)
        slot = lax.rem(high - reader + groups, groups)
        owner = lax.rem(wanted_ref[0, reader * stride + low, slot], groups)
        came = round_of(own_col, owner, groups)
        for at in range(groups):

            @pl.when(came == at)
            def _(at=at, out=out):
                out[...] = held[at][...]


def pick(requests, held, stride):
    groups = len(held)
    return pl.pallas_call(
        functools.partial(pick_kernel, stride),
        out_shape=[jax.ShapeDtypeStruct(held[0].shape, held[0].dtype)] * groups,
        in_specs=[SMEM] + [VMEM] * groups,
        out_specs=[VMEM] * groups,
        name="pick",
    )(requests, *held)


def split_kernel(slots, slab_ref, *rest):
    outs, wide = rest[:-1], rest[-1]
    layers = len(outs)
    rows = slab_ref.shape[0] // layers
    own = lax.axis_index("layer")
    for step, out in enumerate(outs):
        part = target(own, step, layers)
        first = pl.multiple_of(part * rows, rows)
        wide[...] = slab_ref[pl.ds(first, rows)].astype(jnp.float32)
        for slot in range(slots):
            out[slot] = wide[pl.ds(slot, rows // slots, stride=slots)].astype(out.dtype)


def split(slab_tiles, layers):
    high, per, _, slots, side = slab_tiles.shape
    rows = high * per // layers
    flat = slab_tiles.reshape(high * per * slots, side)
    return pl.pallas_call(
        functools.partial(split_kernel, slots),
        out_shape=[jax.ShapeDtypeStruct((slots, rows, side), slab_tiles.dtype)] * layers,
        in_specs=[VMEM],
        out_specs=[VMEM] * layers,
        scratch_shapes=[pltpu.VMEM((rows * slots, side), jnp.float32)],
        name="split",
    )(flat)


def product_kernel(stride, layers, stored, targets_ref, *rest):
    out_ref, tall = rest[-2:]
    lefts, rest = rest[:layers], rest[layers:-2]
    groups = len(rest) // layers
    slots, rows, side = lefts[0].shape
    wanted = targets_ref.shape[2]
    high = lax.axis_index("row") // stride
    left_parts, first_parts, second_parts = [], [], []
    for layer in range(layers):
        for step in range(groups):
            slot = lax.rem(mate(high, step, groups) - high + groups, groups)
            left_parts.append(lefts[layer][slot])
            block = rest[layer * groups + step]
            digits = block[pl.ds(2 * stored * side, id_rows(stored)), :].astype(jnp.float32)
            for part, into in enumerate((first_parts, second_parts)):
                across = [jnp.zeros((side, side), jnp.bfloat16)] * wanted
                for at in range(stored):
                    place = part * stored + at
                    tile = block[pl.ds(place * side, side), :]
                    listed = (
                        digits[2 * place : 2 * place + 1] * (1 << DIGIT)
                        + digits[2 * place + 1 : 2 * place + 2]
                    )
                    for s in range(wanted):
                        goal = targets_ref[0, 0, s].astype(jnp.float32)
                        hit = jnp.broadcast_to(jnp.where(listed == goal, 1.0, 0.0), (side, side))
                        across[s] = across[s] + tile * hit.astype(jnp.bfloat16)
                into.append(jnp.concatenate(across, axis=1))
    left = jnp.concatenate(left_parts, axis=1)
    first = jnp.dot(left, jnp.concatenate(first_parts, axis=0), preferred_element_type=jnp.float32)
    second = jnp.dot(left, jnp.concatenate(second_parts, axis=0), preferred_element_type=jnp.float32)
    summed = 4.0 * first - 3.0 * second
    for s in range(wanted):
        tall[pl.ds(s, rows, stride=wanted)] = summed[:, s * side : (s + 1) * side]
    out_ref[...] = tall[...].astype(out_ref.dtype)


def product(lefts, blocks, targets, stored, stride):
    layers = len(lefts)
    _, rows, side = lefts[0].shape
    wanted = targets.shape[2]
    flat = [block for of_layer in blocks for block in of_layer]
    return pl.pallas_call(
        functools.partial(product_kernel, stride, layers, stored),
        out_shape=jax.ShapeDtypeStruct((rows * wanted, side), lefts[0].dtype),
        in_specs=[SMEM] + [VMEM] * (layers + len(flat)),
        out_specs=VMEM,
        scratch_shapes=[pltpu.VMEM((rows * wanted, side), jnp.float32)],
        compiler_params=pltpu.CompilerParams(vmem_limit_bytes=32 * 1024 * 1024),
        name="product",
    )(targets, *lefts, *flat)


def body(slab_tiles, x_tiles, x_cols, x2_tiles, x2_cols, requests, out_cols):
    layers, rows, groups = (lax.axis_size(axis) for axis in ("layer", "row", "col"))
    stride = rows // groups
    stored = x_tiles.shape[2]
    packed = pack(x_tiles, x2_tiles, x_cols, x2_cols)
    held = [packed[0]] + [exchange(packed[k], "col", k, groups) for k in range(1, groups)]
    lefts = split(slab_tiles, layers)
    lefts = [lefts[0]] + [exchange(lefts[k], "layer", k, layers) for k in range(1, layers)]
    picked = pick(requests, held, stride)
    got = [picked[0]] + [exchange(picked[k], "row", k, groups, stride) for k in range(1, groups)]
    blocks = [got] + [[exchange(block, "layer", k, layers) for block in got] for k in range(1, layers)]
    out = product(lefts, blocks, out_cols, stored, stride)
    high, per = slab_tiles.shape[0] // layers, slab_tiles.shape[1]
    return out.reshape(high, per, 1, out_cols.shape[2], x_tiles.shape[4])


def solution(mesh):
    placed = (
        P(None, "row", "layer", None, None),
        P(("layer", "row", "col"), None, None, None, None),
        P(("layer", "row", "col"), None, None),
        P(("layer", "row", "col"), None, None, None, None),
        P(("layer", "row", "col"), None, None),
        P("layer", None, None),
        P("row", "col", None),
    )
    return jax.shard_map(
        body,
        mesh=mesh,
        in_specs=placed,
        out_specs=P("layer", "row", "col", None, None),
        check_vma=False,
    )
```

time: 93.4 us -> 44 us (0.47)
  between operations: 21.1 us -> 0.02 us
  starting transfers between devices: 29.3 us -> 13.1 us
  waiting for transfers between devices: 29.8 us -> 20.9 us
  local copies, waits for them, and re-layouts: 10.4 us -> 1.62 us
  Pallas kernels: 0 us -> 8.15 us
  matrix products: 2.07 us -> 0 us
    unnamed x2 -> x0, waiting for transfers between devices: 19.8 us -> none
    ppermute x16 -> x11, waiting for transfers between devices: 5.27 us -> 20.9 us  [exchange(): return lax.ppermute(block, axis, route)]
    all_to_all x4 -> x0, starting transfers between devices: 14.3 us -> none  [the longest x1 4.24 us: body(): lax.all_to_all(x_cols, 'col', split_axis=1, concat_axis=0, tiled=True)]
    pallas_call x0 -> x4, Pallas kernels: none -> 8.15 us  [the longest x1 2.3 us: product(): pl.pallas_call(functools.partial(product_kernel, stride, layers, stored),...]
    unnamed x12, local copies, waits for them, and re-layouts: 7.04 us -> 1.62 us
    all_to_all x4 -> x0, waiting for transfers between devices: 4.71 us -> none  [the longest x1 2.7 us: body(): lax.all_to_all(x2_tiles, 'col', split_axis=1, concat_axis=0, tiled=True)]
    dot_general x4 -> x0, matrix products: 2.07 us -> none  [the longest x2 1.09 us: choose_tiles(): jnp.einsum('qus,qubd->qbsd', matches, tile_set, preferred_element_type=jn...]
    ppermute x16 -> x11, starting transfers between devices: 15 us -> 13.1 us  [exchange(): return lax.ppermute(block, axis, route)]
  transfers between devices with their start and end apart: 21 -> 11, of which waited for: 6 -> 7; matrix products, arithmetic and copies ran while one was open for 4% -> 0% of each run, Pallas kernels for 0% -> 4%
where the time goes in v1:
time: 44 us; the launch traced here: 43.8 us
  waiting for transfers between devices  20.9 us (48%)
  starting transfers between devices  13.1 us (30%)
  Pallas kernels  8.15 us (19%)
  local copies, waits for them, and re-layouts  1.62 us (4%)
    ppermute x11, waiting for transfers between devices, exchange(): return lax.ppermute(block, axis, route)  20.9 us
    ppermute x11, starting transfers between devices, exchange(): return lax.ppermute(block, axis, route)  13.1 us
    pallas_call x1, Pallas kernels, product(): pl.pallas_call(functools.partial(product_kernel, stride, layers, stored),...  2.3 us
    pallas_call x1, Pallas kernels, pick(): pl.pallas_call(functools.partial(pick_kernel, stride), out_shape=[jax.Sha...  2.06 us
    pallas_call x1, Pallas kernels, split(): pl.pallas_call(functools.partial(split_kernel, slots), out_shape=[jax.Sha...  1.93 us
    pallas_call x1, Pallas kernels, pack(): pl.pallas_call(pack_kernel, out_shape=[shape] * groups, in_specs=[VMEM, V...  1.86 us
    unnamed x12, local copies, waits for them, and re-layouts  1.62 us
  transfers between devices with their start and end apart: 11, of which 7 were waited for; matrix products, arithmetic and copies ran while one was open for 0% of the time, Pallas kernels for 4%

profile of v1, /device:TPU:0, one launch (start us, length us, event | category | flops | bytes accessed | tf_op | source)
XLA Modules:
  0.0 43.8 jit_solution(1387855387636111683)
XLA Ops:
  0.0 1.9 %pack.1 = (bf16[528,128]{1,0:T(8,128)(2,1)}, bf16[528,128]{1,0:T(8,128)(2,1)}, bf16[528,128]{1,0:T(8,128)(2,1)}, bf16[528,128]{1,0:T(8,128)(2,1)}) custom-call(bf16[1,4,2,128,128]{4,3,2,1,0:T(8,128)(2,1)} %x_ref.1, bf16[1,4,2,128,128]{4,3,2,1,0:T(8,128)(2,1)} %x2_ref.1, s32[1,2,4]{2,1,0:T(2,128)} %bitcast.7, s32[1,2,4]{2,1,0:T(2,128)} %bitcast.8), custom_call_target="tpu_custom_call" | custom-call | tf_op jit(solution)/shard_map/pack/pallas_call | solution.py:60
  1.9 0.5 %collective-permute-start.1 = (bf16[528,128]{1,0:T(8,128)(2,1)}, bf16[528,128]{1,0:T(8,128)(2,1)S(1)}, u32[]{:S(2)}, u32[]{:S(2)}) collective-permute-start(bf16[528,128]{1,0:T(8,128)(2,1)} %get-tuple-element.18), channel_id=1, source_target_pairs={{0,1},{1,0},{2,3},{3,2},{4,5},{5,4},{6,7},{7,6},{8,9},{9,8},{10,11... | collective-permute-start | bytes 405512 | tf_op jit(solution)/shard_map/ppermute | solution.py:32
  2.3 2.5 %collective-permute-start.2 = (bf16[528,128]{1,0:T(8,128)(2,1)}, bf16[528,128]{1,0:T(8,128)(2,1)S(1)}, u32[]{:S(2)}, u32[]{:S(2)}) collective-permute-start(bf16[528,128]{1,0:T(8,128)(2,1)} %get-tuple-element.19), channel_id=1, source_target_pairs={{0,2},{1,3},{2,0},{3,1},{4,6},{5,7},{6,4},{7,5},{8,10},{9,11},{10,... | collective-permute-start | bytes 405512 | tf_op jit(solution)/shard_map/ppermute | solution.py:32
  4.9 0.1 collective-permute-start.3
  5.0 0.0 collective-permute-done.1.rest_1_
  5.0 0.0 copy-start.3
  5.0 4.5 %collective-permute-done.2.rest_2_ = bf16[528,128]{1,0:T(8,128)(2,1)S(1)} collective-permute-done((bf16[528,128]{1,0:T(8,128)(2,1)}, bf16[528,128]{1,0:T(8,128)(2,1)S(1)}, u32[]{:S(2)}, u32[]{:S(2)}) %collective-permute-start.2) | collective-permute-done | bytes 135200 | tf_op jit(solution)/shard_map/ppermute | solution.py:32
  9.5 0.0 copy-start.4
  9.5 2.5 %collective-permute-done.3.rest_3_ = bf16[528,128]{1,0:T(8,128)(2,1)S(1)} collective-permute-done((bf16[528,128]{1,0:T(8,128)(2,1)}, bf16[528,128]{1,0:T(8,128)(2,1)S(1)}, u32[]{:S(2)}, u32[]{:S(2)}) %collective-permute-start.3) | collective-permute-done | bytes 135200 | tf_op jit(solution)/shard_map/ppermute | solution.py:32
  12.0 0.0 copy-start.5
  12.0 0.0 copy-done.3
  12.0 0.0 copy-done.4
  12.0 0.7 %copy-done.5 = bf16[528,128]{1,0:T(8,128)(2,1)} copy-done((bf16[528,128]{1,0:T(8,128)(2,1)}, bf16[528,128]{1,0:T(8,128)(2,1)S(1)}, u32[]{:S(2)}) %copy-start.5) | copy-done | bytes 135192
  12.6 2.1 %pick.1 = (bf16[528,128]{1,0:T(8,128)(2,1)}, bf16[528,128]{1,0:T(8,128)(2,1)}, bf16[528,128]{1,0:T(8,128)(2,1)}, bf16[528,128]{1,0:T(8,128)(2,1)}) custom-call(s32[1,4,4]{2,1,0:T(4,128)} %wanted_ref.1, bf16[528,128]{1,0:T(8,128)(2,1)} %get-tuple-element.17.rest_0_, bf16[528,128]{1,0:T(8,128)(2,1)} %copy-done.3, bf16[528,128]{1,0:T(8,128)(2,1)} %copy-done.4, ...), custom_call_target="tpu_custom_call" | custom-call | tf_op jit(solution)/shard_map/pick/pallas_call | solution.py:88
  14.7 1.6 %collective-permute-start.4 = (bf16[528,128]{1,0:T(8,128)(2,1)}, bf16[528,128]{1,0:T(8,128)(2,1)S(1)}, u32[]{:S(2)}, u32[]{:S(2)}) collective-permute-start(bf16[528,128]{1,0:T(8,128)(2,1)} %get-tuple-element.22), channel_id=1, source_target_pairs={{0,4},{4,0},{8,12},{12,8},{1,5},{5,1},{9,13},{13,9},{2,6},{6,2},{1... | collective-permute-start | bytes 405512 | tf_op jit(solution)/shard_map/ppermute | solution.py:32
  16.3 2.6 %collective-permute-start.5 = (bf16[528,128]{1,0:T(8,128)(2,1)}, bf16[528,128]{1,0:T(8,128)(2,1)S(1)}, u32[]{:S(2)}, u32[]{:S(2)}) collective-permute-start(bf16[528,128]{1,0:T(8,128)(2,1)} %get-tuple-element.23), channel_id=1, source_target_pairs={{0,8},{4,12},{8,0},{12,4},{1,9},{5,13},{9,1},{13,5},{2,10},{6,14},... | collective-permute-start | bytes 405512 | tf_op jit(solution)/shard_map/ppermute | solution.py:32
  18.9 0.2 collective-permute-start.6
  19.1 0.0 copy-start.1
  19.1 1.9 %split.1 = (bf16[4,256,128]{2,1,0:T(8,128)(2,1)}, bf16[4,256,128]{2,1,0:T(8,128)(2,1)}) custom-call(bf16[2048,128]{1,0:T(8,128)(2,1)} %bitcast.6), custom_call_target="tpu_custom_call" | custom-call | tf_op jit(solution)/shard_map/split/pallas_call | solution.py:114
  21.0 1.5 %collective-permute-start = (bf16[4,256,128]{2,1,0:T(8,128)(2,1)}, bf16[4,256,128]{2,1,0:T(8,128)(2,1)S(1)}, u32[]{:S(2)}, u32[]{:S(2)}) collective-permute-start(bf16[4,256,128]{2,1,0:T(8,128)(2,1)} %get-tuple-element.16), channel_id=1, source_target_pairs={{0,16},{16,0},{1,17},{17,1},{2,18},{18,2},{3,19},{19,3},{4,20},{20... | collective-permute-start | bytes 786440 | tf_op jit(solution)/shard_map/ppermute | solution.py:32
  22.5 0.0 copy-done.1
  22.5 0.0 copy-start.2
  22.5 0.5 %collective-permute-start.7 = (bf16[528,128]{1,0:T(8,128)(2,1)S(1)}, bf16[528,128]{1,0:T(8,128)(2,1)S(1)}, u32[]{:S(2)}, u32[]{:S(2)}) collective-permute-start(bf16[528,128]{1,0:T(8,128)(2,1)S(1)} %copy-done.1), channel_id=1, source_target_pairs={{0,16},{16,0},{1,17},{17,1},{2,18},{18,2},{3,19},{19,3},{4,20},{20... | collective-permute-start | bytes 405512 | tf_op jit(solution)/shard_map/ppermute | solution.py:32
  23.0 0.0 collective-permute-done.4.rest_3_
  23.1 1.5 %collective-permute-start.8 = (bf16[528,128]{1,0:T(8,128)(2,1)S(1)}, bf16[528,128]{1,0:T(8,128)(2,1)S(1)}, u32[]{:S(2)}, u32[]{:S(2)}) collective-permute-start(bf16[528,128]{1,0:T(8,128)(2,1)S(1)} %collective-permute-done.4.rest_3_), channel_id=1, source_target_pairs={{0,16},{16,0},{1,17},{17,1},{2,18},{18,2},{3,19},{19,3},{4,20},{20... | collective-permute-start | bytes 405512 | tf_op jit(solution)/shard_map/ppermute | solution.py:32
  24.6 5.1 %collective-permute-done.5.rest_4_ = bf16[528,128]{1,0:T(8,128)(2,1)S(1)} collective-permute-done((bf16[528,128]{1,0:T(8,128)(2,1)}, bf16[528,128]{1,0:T(8,128)(2,1)S(1)}, u32[]{:S(2)}, u32[]{:S(2)}) %collective-permute-start.5) | collective-permute-done | bytes 135200 | tf_op jit(solution)/shard_map/ppermute | solution.py:32
  29.7 1.5 %collective-permute-start.9 = (bf16[528,128]{1,0:T(8,128)(2,1)S(1)}, bf16[528,128]{1,0:T(8,128)(2,1)S(1)}, u32[]{:S(2)}, u32[]{:S(2)}) collective-permute-start(bf16[528,128]{1,0:T(8,128)(2,1)S(1)} %collective-permute-done.5.rest_4_), channel_id=1, source_target_pairs={{0,16},{16,0},{1,17},{17,1},{2,18},{18,2},{3,19},{19,3},{4,20},{20... | collective-permute-start | bytes 405512 | tf_op jit(solution)/shard_map/ppermute | solution.py:32
  31.1 0.0 collective-permute-done.6.rest_5_
  31.2 0.5 %collective-permute-start.10 = (bf16[528,128]{1,0:T(8,128)(2,1)S(1)}, bf16[528,128]{1,0:T(8,128)(2,1)S(1)}, u32[]{:S(2)}, u32[]{:S(2)}) collective-permute-start(bf16[528,128]{1,0:T(8,128)(2,1)S(1)} %collective-permute-done.6.rest_5_), channel_id=1, source_target_pairs={{0,16},{16,0},{1,17},{17,1},{2,18},{18,2},{3,19},{19,3},{4,20},{20... | collective-permute-start | bytes 405512 | tf_op jit(solution)/shard_map/ppermute | solution.py:32
  31.7 0.0 collective-permute-done.rest_1_
  31.7 1.7 %collective-permute-done.7.rest_6_ = bf16[528,128]{1,0:T(8,128)(2,1)S(1)} collective-permute-done((bf16[528,128]{1,0:T(8,128)(2,1)S(1)}, bf16[528,128]{1,0:T(8,128)(2,1)S(1)}, u32[]{:S(2)}, u32[]{:S(2)}) %collective-permute-start.7) | collective-permute-done | bytes 135200 | tf_op jit(solution)/shard_map/ppermute | solution.py:32
  33.4 2.9 %collective-permute-done.8.rest_7_ = bf16[528,128]{1,0:T(8,128)(2,1)S(1)} collective-permute-done((bf16[528,128]{1,0:T(8,128)(2,1)S(1)}, bf16[528,128]{1,0:T(8,128)(2,1)S(1)}, u32[]{:S(2)}, u32[]{:S(2)}) %collective-permute-start.8) | collective-permute-done | bytes 135200 | tf_op jit(solution)/shard_map/ppermute | solution.py:32
  36.3 2.8 %collective-permute-done.9.rest_8_ = bf16[528,128]{1,0:T(8,128)(2,1)S(1)} collective-permute-done((bf16[528,128]{1,0:T(8,128)(2,1)S(1)}, bf16[528,128]{1,0:T(8,128)(2,1)S(1)}, u32[]{:S(2)}, u32[]{:S(2)}) %collective-permute-start.9) | collective-permute-done | bytes 135200 | tf_op jit(solution)/shard_map/ppermute | solution.py:32
  39.1 1.4 %collective-permute-done.10.rest_9_ = bf16[528,128]{1,0:T(8,128)(2,1)S(1)} collective-permute-done((bf16[528,128]{1,0:T(8,128)(2,1)S(1)}, bf16[528,128]{1,0:T(8,128)(2,1)S(1)}, u32[]{:S(2)}, u32[]{:S(2)}) %collective-permute-start.10) | collective-permute-done | bytes 135200 | tf_op jit(solution)/shard_map/ppermute | solution.py:32
  40.5 0.0 copy-done.2
  40.5 0.0 copy-start
  40.5 0.9 %copy-done = bf16[4,256,128]{2,1,0:T(8,128)(2,1)S(1)} copy-done((bf16[4,256,128]{2,1,0:T(8,128)(2,1)S(1)}, bf16[4,256,128]{2,1,0:T(8,128)(2,1)}, u32[]{:S(2)}) %copy-start) | copy-done | bytes 262168
  41.5 2.3 %product.1 = bf16[1024,128]{1,0:T(8,128)(2,1)} custom-call(s32[1,1,4]{2,1,0:T(1,128)S(1)} %copy-done.2, bf16[4,256,128]{2,1,0:T(8,128)(2,1)S(1)} %copy-done, bf16[4,256,128]{2,1,0:T(8,128)(2,1)S(1)} %collective-permute-done.rest_1_, bf16[528,128]{1,0:T(8,128)(2,1)S(1)} %copy-done.1, bf16[528,128]{1,0:T(8,128)(2,1)S(1)} %collective-permute-done.4.rest_3_, ...), custom_call_target="tpu_custom_call" | custom-call | tf_op jit(solution)/shard_map/product/pallas_call | solution.py:166
Async XLA Ops:
  1.9 3.1 %collective-permute-start.1 = (bf16[528,128]{1,0:T(8,128)(2,1)}, bf16[528,128]{1,0:T(8,128)(2,1)S(1)}, u32[]{:S(2)}, u32[]{:S(2)}) collective-permute-start(bf16[528,128]{1,0:T(8,128)(2,1)} %get-tuple-element.18), channel_id=1, source_target_pairs={{0,1},{1,0},{2,3},{3,2},{4,5},{5,4},{6,7},{7,6},{8,9},{9,8},{10,11... | collective-permute-start | bytes 405512 | tf_op jit(solution)/shard_map/ppermute | solution.py:32
  2.3 7.2 %collective-permute-start.2 = (bf16[528,128]{1,0:T(8,128)(2,1)}, bf16[528,128]{1,0:T(8,128)(2,1)S(1)}, u32[]{:S(2)}, u32[]{:S(2)}) collective-permute-start(bf16[528,128]{1,0:T(8,128)(2,1)} %get-tuple-element.19), channel_id=1, source_target_pairs={{0,2},{1,3},{2,0},{3,1},{4,6},{5,7},{6,4},{7,5},{8,10},{9,11},{10,... | collective-permute-start | bytes 405512 | tf_op jit(solution)/shard_map/ppermute | solution.py:32
  4.9 7.1 %collective-permute-start.3 = (bf16[528,128]{1,0:T(8,128)(2,1)}, bf16[528,128]{1,0:T(8,128)(2,1)S(1)}, u32[]{:S(2)}, u32[]{:S(2)}) collective-permute-start(bf16[528,128]{1,0:T(8,128)(2,1)} %get-tuple-element.20), channel_id=1, source_target_pairs={{0,3},{1,2},{2,1},{3,0},{4,7},{5,6},{6,5},{7,4},{8,11},{9,10},{10,... | collective-permute-start | bytes 405512 | tf_op jit(solution)/shard_map/ppermute | solution.py:32
  5.0 7.0 %copy-start.3 = (bf16[528,128]{1,0:T(8,128)(2,1)}, bf16[528,128]{1,0:T(8,128)(2,1)S(1)}, u32[]{:S(2)}) copy-start(bf16[528,128]{1,0:T(8,128)(2,1)S(1)} %collective-permute-done.1.rest_1_) | copy-start | bytes 405508
  9.5 2.5 %copy-start.4 = (bf16[528,128]{1,0:T(8,128)(2,1)}, bf16[528,128]{1,0:T(8,128)(2,1)S(1)}, u32[]{:S(2)}) copy-start(bf16[528,128]{1,0:T(8,128)(2,1)S(1)} %collective-permute-done.2.rest_2_) | copy-start | bytes 405508
  12.0 0.7 %copy-start.5 = (bf16[528,128]{1,0:T(8,128)(2,1)}, bf16[528,128]{1,0:T(8,128)(2,1)S(1)}, u32[]{:S(2)}) copy-start(bf16[528,128]{1,0:T(8,128)(2,1)S(1)} %collective-permute-done.3.rest_3_) | copy-start | bytes 405508
  14.7 8.4 %collective-permute-start.4 = (bf16[528,128]{1,0:T(8,128)(2,1)}, bf16[528,128]{1,0:T(8,128)(2,1)S(1)}, u32[]{:S(2)}, u32[]{:S(2)}) collective-permute-start(bf16[528,128]{1,0:T(8,128)(2,1)} %get-tuple-element.22), channel_id=1, source_target_pairs={{0,4},{4,0},{8,12},{12,8},{1,5},{5,1},{9,13},{13,9},{2,6},{6,2},{1... | collective-permute-start | bytes 405512 | tf_op jit(solution)/shard_map/ppermute | solution.py:32
  16.3 13.4 %collective-permute-start.5 = (bf16[528,128]{1,0:T(8,128)(2,1)}, bf16[528,128]{1,0:T(8,128)(2,1)S(1)}, u32[]{:S(2)}, u32[]{:S(2)}) collective-permute-start(bf16[528,128]{1,0:T(8,128)(2,1)} %get-tuple-element.23), channel_id=1, source_target_pairs={{0,8},{4,12},{8,0},{12,4},{1,9},{5,13},{9,1},{13,5},{2,10},{6,14},... | collective-permute-start | bytes 405512 | tf_op jit(solution)/shard_map/ppermute | solution.py:32
  18.9 12.3 %collective-permute-start.6 = (bf16[528,128]{1,0:T(8,128)(2,1)}, bf16[528,128]{1,0:T(8,128)(2,1)S(1)}, u32[]{:S(2)}, u32[]{:S(2)}) collective-permute-start(bf16[528,128]{1,0:T(8,128)(2,1)} %get-tuple-element.24), channel_id=1, source_target_pairs={{0,12},{4,8},{8,4},{12,0},{1,13},{5,9},{9,5},{13,1},{2,14},{6,10},... | collective-permute-start | bytes 405512 | tf_op jit(solution)/shard_map/ppermute | solution.py:32
  19.1 3.4 %copy-start.1 = (bf16[528,128]{1,0:T(8,128)(2,1)S(1)}, bf16[528,128]{1,0:T(8,128)(2,1)}, u32[]{:S(2)}) copy-start(bf16[528,128]{1,0:T(8,128)(2,1)} %get-tuple-element.21.rest_2_) | copy-start | bytes 405508
  21.0 10.7 %collective-permute-start = (bf16[4,256,128]{2,1,0:T(8,128)(2,1)}, bf16[4,256,128]{2,1,0:T(8,128)(2,1)S(1)}, u32[]{:S(2)}, u32[]{:S(2)}) collective-permute-start(bf16[4,256,128]{2,1,0:T(8,128)(2,1)} %get-tuple-element.16), channel_id=1, source_target_pairs={{0,16},{16,0},{1,17},{17,1},{2,18},{18,2},{3,19},{19,3},{4,20},{20... | collective-permute-start | bytes 786440 | tf_op jit(solution)/shard_map/ppermute | solution.py:32
  22.5 18.0 %copy-start.2 = (s32[1,1,4]{2,1,0:T(1,128)S(1)}, s32[1,1,4]{2,1,0:T(1,128)}, u32[]{:S(2)}) copy-start(s32[1,1,4]{2,1,0:T(1,128)} %targets_ref.1) | copy-start | bytes 52
  22.5 10.8 %collective-permute-start.7 = (bf16[528,128]{1,0:T(8,128)(2,1)S(1)}, bf16[528,128]{1,0:T(8,128)(2,1)S(1)}, u32[]{:S(2)}, u32[]{:S(2)}) collective-permute-start(bf16[528,128]{1,0:T(8,128)(2,1)S(1)} %copy-done.1), channel_id=1, source_target_pairs={{0,16},{16,0},{1,17},{17,1},{2,18},{18,2},{3,19},{19,3},{4,20},{20... | collective-permute-start | bytes 405512 | tf_op jit(solution)/shard_map/ppermute | solution.py:32
  23.1 13.2 %collective-permute-start.8 = (bf16[528,128]{1,0:T(8,128)(2,1)S(1)}, bf16[528,128]{1,0:T(8,128)(2,1)S(1)}, u32[]{:S(2)}, u32[]{:S(2)}) collective-permute-start(bf16[528,128]{1,0:T(8,128)(2,1)S(1)} %collective-permute-done.4.rest_3_), channel_id=1, source_target_pairs={{0,16},{16,0},{1,17},{17,1},{2,18},{18,2},{3,19},{19,3},{4,20},{20... | collective-permute-start | bytes 405512 | tf_op jit(solution)/shard_map/ppermute | solution.py:32
  29.7 9.4 %collective-permute-start.9 = (bf16[528,128]{1,0:T(8,128)(2,1)S(1)}, bf16[528,128]{1,0:T(8,128)(2,1)S(1)}, u32[]{:S(2)}, u32[]{:S(2)}) collective-permute-start(bf16[528,128]{1,0:T(8,128)(2,1)S(1)} %collective-permute-done.5.rest_4_), channel_id=1, source_target_pairs={{0,16},{16,0},{1,17},{17,1},{2,18},{18,2},{3,19},{19,3},{4,20},{20... | collective-permute-start | bytes 405512 | tf_op jit(solution)/shard_map/ppermute | solution.py:32
  31.2 9.4 %collective-permute-start.10 = (bf16[528,128]{1,0:T(8,128)(2,1)S(1)}, bf16[528,128]{1,0:T(8,128)(2,1)S(1)}, u32[]{:S(2)}, u32[]{:S(2)}) collective-permute-start(bf16[528,128]{1,0:T(8,128)(2,1)S(1)} %collective-permute-done.6.rest_5_), channel_id=1, source_target_pairs={{0,16},{16,0},{1,17},{17,1},{2,18},{18,2},{3,19},{19,3},{4,20},{20... | collective-permute-start | bytes 405512 | tf_op jit(solution)/shard_map/ppermute | solution.py:32
  40.5 1.0 %copy-start = (bf16[4,256,128]{2,1,0:T(8,128)(2,1)S(1)}, bf16[4,256,128]{2,1,0:T(8,128)(2,1)}, u32[]{:S(2)}) copy-start(bf16[4,256,128]{2,1,0:T(8,128)(2,1)} %get-tuple-element.15.rest_0_) | copy-start | bytes 786436

commit v2 on v1

v2 whole, which is shorter than its diff:
```python
import functools

import jax
import jax.numpy as jnp
from jax import lax
from jax.experimental import pallas as pl
from jax.experimental.pallas import tpu as pltpu
from jax.sharding import PartitionSpec as P

DIGIT = 8
VMEM = pl.BlockSpec(memory_space=pltpu.VMEM)
SMEM = pl.BlockSpec(memory_space=pltpu.SMEM)
HBM = pl.BlockSpec(memory_space=pltpu.HBM)
SMALL = pltpu.CompilerParams(vmem_limit_bytes=8 * 1024 * 1024)


def mate(index, step, size):
    return index ^ step if size & (size - 1) == 0 else (index - step) % size


def target(index, step, size):
    return index ^ step if size & (size - 1) == 0 else (index + step) % size


def round_of(index, source, size):
    return index ^ source if size & (size - 1) == 0 else lax.rem(index - source + size, size)


def exchange(block, axis, step, size, stride=1):
    route = []
    for place in range(size * stride):
        high, low = divmod(place, stride)
        route.append((place, target(high, step, size) * stride + low))
    return lax.ppermute(block, axis, route)


def id_rows(stored):
    return -(-4 * stored // 16) * 16


def pack_kernel(stride, x_far, x2_far, *rest):
    groups, stored, side = x_far.shape[1:4]
    fars, outs, (choice, goals) = rest[:4], rest[4 : 4 + groups], rest[4 + groups : 6 + groups]
    nears, (sems, id_sems) = rest[6 + groups : 10 + groups], rest[10 + groups :]
    cols_ref, cols2_ref, wanted_ref, goals_ref = nears
    own = lax.axis_index("col")
    ids = [
        pltpu.make_async_copy(far, near, id_sems.at[at]) for at, (far, near) in enumerate(zip(fars, nears))
    ]
    loads = [
        pltpu.make_async_copy(
            far.at[0, target(own, step, groups), at],
            out.at[pl.ds((part * stored + at) * side, side)],
            sems.at[step, part * stored + at],
        )
        for step, out in enumerate(outs)
        for part, far in enumerate((x_far, x2_far))
        for at in range(stored)
    ]
    for load in ids + loads:
        load.start()
    for load in ids:
        load.wait()
    count = id_rows(stored)
    row = lax.broadcasted_iota(jnp.int32, (count, side), 0)
    for step, out in enumerate(outs):
        reader = target(own, step, groups)
        digits = jnp.zeros((count, side), jnp.int32)
        for part, cols in enumerate((cols_ref, cols2_ref)):
            for at in range(stored):
                value, place = cols[0, at, reader], 2 * (part * stored + at)
                digits = jnp.where(row == place, value >> DIGIT, digits)
                digits = jnp.where(row == place + 1, value & ((1 << DIGIT) - 1), digits)
        out[pl.ds(2 * stored * side, count), :] = digits.astype(jnp.float32).astype(out.dtype)
    own_row = lax.axis_index("row")
    high, low = own_row // stride, own_row % stride
    row = lax.broadcasted_iota(jnp.int32, choice.shape, 0)
    came = jnp.zeros(choice.shape, jnp.int32)
    for step in range(groups):
        reader = target(high, step, groups)
        slot = lax.rem(high - reader + groups, groups)
        owner = lax.rem(wanted_ref[0, reader * stride + low, slot], groups)
        came = jnp.where(row // groups == step, round_of(own, owner, groups), came)
    choice[...] = jnp.where(row % groups == came, 1.0, 0.0)
    row = lax.broadcasted_iota(jnp.int32, goals.shape, 0)
    goal = jnp.zeros(goals.shape, jnp.int32)
    for s in range(goals_ref.shape[2]):
        goal = jnp.where(row == s, goals_ref[0, 0, s], goal)
    goals[...] = goal.astype(jnp.float32)
    for load in loads:
        load.wait()


def pinned(array):
    return pltpu.with_memory_space_constraint(array, pltpu.HBM)


def pack(x_tiles, x2_tiles, x_cols, x2_cols, requests, out_cols, stride):
    _, groups, stored, side, _ = x_tiles.shape
    kind = x_tiles.dtype
    small = (jnp.swapaxes(x_cols, 1, 2), jnp.swapaxes(x2_cols, 1, 2), requests, out_cols)
    out = pl.pallas_call(
        functools.partial(pack_kernel, stride),
        out_shape=[jax.ShapeDtypeStruct((2 * stored * side + id_rows(stored), side), kind)] * groups
        + [
            jax.ShapeDtypeStruct((groups * groups, side), jnp.float32),
            jax.ShapeDtypeStruct((-(-out_cols.shape[2] // 8) * 8, side), jnp.float32),
        ],
        in_specs=[HBM] * 6,
        out_specs=[VMEM] * (groups + 2),
        scratch_shapes=[pltpu.SMEM(array.shape, array.dtype) for array in small]
        + [pltpu.SemaphoreType.DMA((groups, 2 * stored)), pltpu.SemaphoreType.DMA((len(small),))],
        compiler_params=SMALL,
        name="pack",
    )(pinned(x_tiles), pinned(x2_tiles), *map(pinned, small))
    return list(out[:groups]), *out[groups:]


def split_kernel(slots, slab_far, _, own_ref, *rest):
    outs, (wide, slab_ref, sems) = rest[:-3], rest[-3:]
    layers, pieces = len(outs) + 1, sems.shape[0]
    rows = slab_far.shape[0] // layers
    share = rows // pieces
    own, parity = lax.axis_index("layer"), lax.axis_index("col") % 2
    firsts = [target(own, step, layers) * rows for step in range(layers)]
    loads = [
        [
            pltpu.make_async_copy(
                slab_far.at[pl.ds(pl.multiple_of(first + at * share, share), share)],
                slab_ref.at[step, pl.ds(at * share, share)],
                sems.at[at, step],
            )
            for at in range(pieces)
        ]
        for step, first in enumerate(firsts)
    ]
    for load in sum(loads, []):
        load.start()
    for step in reversed(range(layers)):
        for load in loads[step]:
            load.wait()
        wide[...] = slab_ref[step].astype(jnp.float32)
        if step:
            half = slots // 2
            for slot in range(half):
                picked = wide[pl.ds(parity * half + slot, rows // slots, stride=slots)]
                outs[step - 1][slot] = picked.astype(own_ref.dtype)
        else:
            for slot in range(slots):
                own_ref[slot] = wide[pl.ds(slot, rows // slots, stride=slots)].astype(own_ref.dtype)


def split(slab_tiles, after, layers):
    high, per, _, slots, side = slab_tiles.shape
    rows = high * per // layers
    kind = slab_tiles.dtype
    out = pl.pallas_call(
        functools.partial(split_kernel, slots),
        out_shape=[jax.ShapeDtypeStruct((slots, rows, side), kind)]
        + [jax.ShapeDtypeStruct((slots // 2, rows, side), kind)] * (layers - 1),
        in_specs=[HBM, pl.BlockSpec(memory_space=pl.ANY)],
        out_specs=[VMEM] * layers,
        scratch_shapes=[
            pltpu.VMEM((rows * slots, side), jnp.float32),
            pltpu.VMEM((layers, rows * slots, side), kind),
            pltpu.SemaphoreType.DMA((4, layers)),
        ],
        compiler_params=SMALL,
        name="split",
    )(pinned(slab_tiles.reshape(high * per * slots, side)), after)
    return out[0], list(out[1:])


def pick_kernel(cuts, choice, *rest):
    groups = len(cuts)
    held, outs = rest[:groups], list(rest[groups:])
    side = choice.shape[1]
    for step, sizes in enumerate(cuts):
        first = 0
        for size in sizes:
            out = outs.pop(0)
            total = jnp.zeros((size, side), out.dtype)
            for at in range(groups):
                place = step * groups + at
                hit = jnp.broadcast_to(choice[place : place + 1, :], (size, side)).astype(out.dtype)
                total += held[at][pl.ds(first, size), :] * hit
            out[...] = total
            first += size


def pick(choice, held, cuts):
    side, kind = held[0].shape[1], held[0].dtype
    sizes = [size for cut in cuts for size in cut]
    out = pl.pallas_call(
        functools.partial(pick_kernel, cuts),
        out_shape=[jax.ShapeDtypeStruct((size, side), kind) for size in sizes],
        in_specs=[VMEM] * (1 + len(held)),
        out_specs=[VMEM] * len(sizes),
        compiler_params=SMALL,
        name="pick",
    )(choice, *held)
    out = iter(out)
    return [[next(out) for _ in cut] for cut in cuts]


def product_kernel(stride, layers, stored, rounds, cuts, wanted, last, goals, *rest):
    lefts, rest = rest[: 2 * layers - 1], list(rest[2 * layers - 1 :])
    groups = len(cuts)
    slots, rows, side = lefts[0].shape
    half = slots // 2
    high, parity = lax.axis_index("row") // stride, lax.axis_index("col") % 2
    left_parts, sums = [], ([], [])
    for layer in range(layers):
        for step in rounds:
            slot = lax.rem(mate(high, step, groups) - high + groups, groups)
            if layer:
                same, other = lefts[2 * layer - 1], lefts[2 * layer]
                at = lax.rem(slot, half)
                left_parts.append(jnp.where(slot // half == parity, same[at], other[at]))
            else:
                left_parts.append(lefts[0][slot])
            pieces, rest = rest[: len(cuts[step])], rest[len(cuts[step]) :]

            def fetch(first, size, pieces=pieces):
                for piece in pieces:
                    if first < piece.shape[0]:
                        return piece[pl.ds(first, size), :]
                    first -= piece.shape[0]

            digits = fetch(2 * stored * side, id_rows(stored)).astype(jnp.float32)
            for part, into in enumerate(sums):
                across = [jnp.zeros((side, side), jnp.bfloat16)] * wanted
                for at in range(stored):
                    place = part * stored + at
                    tile = fetch(place * side, side)
                    listed = (
                        digits[2 * place : 2 * place + 1] * (1 << DIGIT)
                        + digits[2 * place + 1 : 2 * place + 2]
                    )
                    for s in range(wanted):
                        hit = jnp.where(listed == goals[s : s + 1, :], 1.0, 0.0)
                        hit = jnp.broadcast_to(hit, (side, side))
                        across[s] = across[s] + tile * hit.astype(jnp.bfloat16)
                into.append(jnp.concatenate(across, axis=1))
    left = jnp.concatenate(left_parts, axis=1)
    first, second = (
        jnp.dot(left, jnp.concatenate(chosen, axis=0), preferred_element_type=jnp.float32) for chosen in sums
    )
    summed = 4.0 * first - 3.0 * second
    if last:
        tall = rest.pop()
    out_ref = rest.pop()
    if rest:
        summed += rest.pop()[...]
    if last:
        for s in range(wanted):
            tall[pl.ds(s, rows, stride=wanted)] = summed[:, s * side : (s + 1) * side]
        summed = tall[...]
    out_ref[...] = summed.astype(out_ref.dtype)


def product(lefts, blocks, total, goals, wanted, stored, stride, rounds, cuts, last):
    layers = len(blocks)
    _, rows, side = lefts[0].shape
    flat = [piece for of_layer in blocks for step in rounds for piece in of_layer[step]]
    flat += [] if total is None else [total]
    shape = (rows * wanted, side) if last else (rows, wanted * side)
    return pl.pallas_call(
        functools.partial(product_kernel, stride, layers, stored, rounds, cuts, wanted, last),
        out_shape=jax.ShapeDtypeStruct(shape, lefts[0].dtype if last else jnp.float32),
        in_specs=[VMEM] * (1 + len(lefts) + len(flat)),
        out_specs=VMEM,
        scratch_shapes=[pltpu.VMEM(shape, jnp.float32)] if last else [],
        compiler_params=pltpu.CompilerParams(vmem_limit_bytes=16 * 1024 * 1024),
        name="product",
    )(goals, *lefts, *flat)


def body(slab_tiles, x_tiles, x_cols, x2_tiles, x2_cols, requests, out_cols):
    layers, rows, groups = (lax.axis_size(axis) for axis in ("layer", "row", "col"))
    stride = rows // groups
    _, _, stored, side, _ = x_tiles.shape
    half, whole = stored * side, 2 * stored * side + id_rows(stored)
    order = [0, *reversed(range(3, groups)), 1, 2]
    cuts = [(half, whole - half) if k == order[-1] else (whole,) for k in range(groups)]
    packed, choice, goals = pack(x_tiles, x2_tiles, x_cols, x2_cols, requests, out_cols, stride)
    held = [packed[0]] + [exchange(packed[k], "col", k, groups) for k in range(1, groups)]
    own, sent = split(slab_tiles, held[1], layers)
    lefts = [exchange(sent[k - 1], "layer", k, layers) for k in range(1, layers)]
    held, lefts = lax.optimization_barrier((held, lefts))
    lefts = [own] + [left for same in lefts for left in (same, exchange(same, "col", 1, groups))]
    picked = pick(choice, held, cuts)
    got = [picked[0]] + [None] * (groups - 1)
    for k in order[1:]:
        got[k] = [exchange(piece, "row", k, groups, stride) for piece in picked[k]]
    blocks = [got] + [[None] * groups for _ in range(1, layers)]

    def forward(k, after):
        mine, _ = lax.optimization_barrier((got[k], after))
        for step in range(1, layers):
            blocks[step][k] = [exchange(piece, "layer", step, layers) for piece in mine]

    def add(total, rounds, last):
        return product(lefts, blocks, total, goals, out_cols.shape[2], stored, stride, rounds, cuts, last)

    forward(0, ())
    for k in order[1:]:
        forward(k, blocks[-1][0])
    total = add(None, order[:2], False)
    for k in order[2:-1]:
        total = add(total, [k], False)
    total = add(total, order[-1:], True)
    high, per = slab_tiles.shape[0] // layers, slab_tiles.shape[1]
    return total.reshape(high, per, 1, out_cols.shape[2], side)


def solution(mesh):
    placed = (
        P(None, "row", "layer", None, None),
        P(("layer", "row", "col"), None, None, None, None),
        P(("layer", "row", "col"), None, None),
        P(("layer", "row", "col"), None, None, None, None),
        P(("layer", "row", "col"), None, None),
        P("layer", None, None),
        P("row", "col", None),
    )
    return jax.shard_map(
        body,
        mesh=mesh,
        in_specs=placed,
        out_specs=P("layer", "row", "col", None, None),
        check_vma=False,
    )
```

time: 44 us -> 34.5 us (0.78)
  waiting for transfers between devices: 20.9 us -> 11.1 us
  starting transfers between devices: 13.1 us -> 18.2 us
  Pallas kernels: 8.15 us -> 4.89 us
  local copies, waits for them, and re-layouts: 1.62 us -> 0 us
    ppermute x11 -> x14, waiting for transfers between devices: 20.9 us -> 11.1 us  [exchange(): return lax.ppermute(block, axis, route)]
    ppermute x11 -> x14, starting transfers between devices: 13.1 us -> 18.2 us  [exchange(): return lax.ppermute(block, axis, route)]
    pallas_call x3 -> x5, Pallas kernels: 6.22 us -> 3.62 us  [the longest x3 2.13 us: product(): pl.pallas_call(functools.partial(product_kernel, stride, layers, stored,...]
    unnamed x12 -> x0, local copies, waits for them, and re-layouts: 1.62 us -> none
    pallas_call x1, Pallas kernels: 1.93 us -> 1.27 us  [split(): pl.pallas_call(functools.partial(split_kernel, slots), out_shape=[jax.Sha...]
  transfers between devices with their start and end apart: 11 -> 14, of which waited for: 7 -> 7; matrix products, arithmetic and copies ran while one was open for 0% -> 0% of each run, Pallas kernels for 4% -> 7%
where the time goes in v2:
time: 34.5 us; the launch traced here: 34.2 us
  starting transfers between devices  18.2 us (53%)
  waiting for transfers between devices  11.1 us (32%)
  Pallas kernels  4.89 us (14%)
    ppermute x14, starting transfers between devices, exchange(): return lax.ppermute(block, axis, route)  18.2 us
    ppermute x14, waiting for transfers between devices, exchange(): return lax.ppermute(block, axis, route)  11.1 us
    pallas_call x3, Pallas kernels, product(): pl.pallas_call(functools.partial(product_kernel, stride, layers, stored,...  2.13 us
    pallas_call x1, Pallas kernels, split(): pl.pallas_call(functools.partial(split_kernel, slots), out_shape=[jax.Sha...  1.27 us
    pallas_call x1, Pallas kernels, pack(): pl.pallas_call(functools.partial(pack_kernel, stride), out_shape=[jax.Sha...  1.17 us
  transfers between devices with their start and end apart: 14, of which 7 were waited for; matrix products, arithmetic and copies ran while one was open for 0% of the time, Pallas kernels for 7%

profile of v2, /device:TPU:0, one launch (start us, length us, event | category | flops | bytes accessed | tf_op | source)
XLA Modules:
  0.0 34.2 jit_solution(1910996234788273680)
XLA Ops:
  0.0 1.2 %pack.1 = (bf16[528,128]{1,0:T(8,128)(2,1)S(1)}, bf16[528,128]{1,0:T(8,128)(2,1)S(1)}, bf16[528,128]{1,0:T(8,128)(2,1)S(1)}, bf16[528,128]{1,0:T(8,128)(2,1)S(1)...) custom-call(bf16[1,4,2,128,128]{4,3,2,1,0:T(8,128)(2,1)} %x_far.1, bf16[1,4,2,128,128]{4,3,2,1,0:T(8,128)(2,1)} %x2_far.1, ...), custom_call_target="tpu_custom_call" | custom-call | tf_op jit(solution)/shard_map/pack/pallas_call | solution.py:102
  1.2 0.5 %collective-permute-start = (bf16[528,128]{1,0:T(8,128)(2,1)S(1)}, bf16[528,128]{1,0:T(8,128)(2,1)S(1)}, u32[]{:S(2)}, u32[]{:S(2)}) collective-permute-start(bf16[528,128]{1,0:T(8,128)(2,1)S(1)} %get-tuple-element.28), channel_id=1, source_target_pairs={{0,1},{1,0},{2,3},{3,2},{4,5},{5,4},{6,7},{7,6},{8,9},{9,8},{10,11... | collective-permute-start | bytes 405512 | tf_op jit(solution)/shard_map/ppermute | solution.py:34
  1.7 2.6 %collective-permute-start.1 = (bf16[528,128]{1,0:T(8,128)(2,1)S(1)}, bf16[528,128]{1,0:T(8,128)(2,1)S(1)}, u32[]{:S(2)}, u32[]{:S(2)}) collective-permute-start(bf16[528,128]{1,0:T(8,128)(2,1)S(1)} %get-tuple-element.31), channel_id=1, source_target_pairs={{0,2},{1,3},{2,0},{3,1},{4,6},{5,7},{6,4},{7,5},{8,10},{9,11},{10,... | collective-permute-start | bytes 405512 | tf_op jit(solution)/shard_map/ppermute | solution.py:34
  4.3 0.1 collective-permute-start.2
  4.4 0.0 collective-permute-done._.rest_1_
  4.4 1.3 %split.1 = (bf16[4,256,128]{2,1,0:T(8,128)(2,1)S(1)}, bf16[2,256,128]{2,1,0:T(8,128)(2,1)S(1)}) custom-call(bf16[2048,128]{1,0:T(8,128)(2,1)} %bitcast.6, bf16[528,128]{1,0:T(8,128)(2,1)S(1)} %collective-permute-done._.rest_1_), custom_call_target="tpu_custom_call" | custom-call | tf_op jit(solution)/shard_map/split/pallas_call | solution.py:157
  5.6 1.8 %collective-permute-start.3 = (bf16[2,256,128]{2,1,0:T(8,128)(2,1)S(1)}, bf16[2,256,128]{2,1,0:T(8,128)(2,1)S(1)}, u32[]{:S(2)}, u32[]{:S(2)}) collective-permute-start(bf16[2,256,128]{2,1,0:T(8,128)(2,1)S(1)} %get-tuple-element.33), channel_id=1, source_target_pairs={{0,16},{16,0},{1,17},{17,1},{2,18},{18,2},{3,19},{19,3},{4,20},{20... | collective-permute-start | bytes 393224 | tf_op jit(solution)/shard_map/ppermute | solution.py:34
  7.4 1.3 %collective-permute-done.1.rest_2_ = bf16[528,128]{1,0:T(8,128)(2,1)S(1)} collective-permute-done((bf16[528,128]{1,0:T(8,128)(2,1)S(1)}, bf16[528,128]{1,0:T(8,128)(2,1)S(1)}, u32[]{:S(2)}, u32[]{:S(2)}) %collective-permute-start.1) | collective-permute-done | bytes 135200 | tf_op jit(solution)/shard_map/ppermute | solution.py:34
  8.7 2.4 %collective-permute-done.2.rest_3_ = bf16[528,128]{1,0:T(8,128)(2,1)S(1)} collective-permute-done((bf16[528,128]{1,0:T(8,128)(2,1)S(1)}, bf16[528,128]{1,0:T(8,128)(2,1)S(1)}, u32[]{:S(2)}, u32[]{:S(2)}) %collective-permute-start.2) | collective-permute-done | bytes 135200 | tf_op jit(solution)/shard_map/ppermute | solution.py:34
  11.1 0.3 collective-permute-done.3.rest_1_
  11.4 0.3 pick.1
  11.7 3.9 %collective-permute-start.12 = (bf16[528,128]{1,0:T(8,128)(2,1)S(1)}, bf16[528,128]{1,0:T(8,128)(2,1)S(1)}, u32[]{:S(2)}, u32[]{:S(2)}) collective-permute-start(bf16[528,128]{1,0:T(8,128)(2,1)S(1)} %get-tuple-element.47), channel_id=1, source_target_pairs={{0,12},{4,8},{8,4},{12,0},{1,13},{5,9},{9,5},{13,1},{2,14},{6,10},... | collective-permute-start | bytes 405512 | tf_op jit(solution)/shard_map/ppermute | solution.py:34
  15.6 1.5 %collective-permute-start.7 = (bf16[528,128]{1,0:T(8,128)(2,1)S(1)}, bf16[528,128]{1,0:T(8,128)(2,1)S(1)}, u32[]{:S(2)}, u32[]{:S(2)}) collective-permute-start(bf16[528,128]{1,0:T(8,128)(2,1)S(1)} %get-tuple-element.42.rest_3_), channel_id=1, source_target_pairs={{0,16},{16,0},{1,17},{17,1},{2,18},{18,2},{3,19},{19,3},{4,20},{20... | collective-permute-start | bytes 405512 | tf_op jit(solution)/shard_map/ppermute | solution.py:34
  17.1 0.0 collective-permute-start.10
  17.1 0.8 %collective-permute-start.6 = (bf16[272,128]{1,0:T(8,128)(2,1)S(1)}, bf16[272,128]{1,0:T(8,128)(2,1)S(1)}, u32[]{:S(2)}, u32[]{:S(2)}) collective-permute-start(bf16[272,128]{1,0:T(8,128)(2,1)S(1)} %get-tuple-element.41), channel_id=1, source_target_pairs={{0,8},{4,12},{8,0},{12,4},{1,9},{5,13},{9,1},{13,5},{2,10},{6,14},... | collective-permute-start | bytes 208904 | tf_op jit(solution)/shard_map/ppermute | solution.py:34
  17.9 2.1 %collective-permute-start.5 = (bf16[256,128]{1,0:T(8,128)(2,1)S(1)}, bf16[256,128]{1,0:T(8,128)(2,1)S(1)}, u32[]{:S(2)}, u32[]{:S(2)}) collective-permute-start(bf16[256,128]{1,0:T(8,128)(2,1)S(1)} %get-tuple-element.40), channel_id=1, source_target_pairs={{0,8},{4,12},{8,0},{12,4},{1,9},{5,13},{9,1},{13,5},{2,10},{6,14},... | collective-permute-start | bytes 196616 | tf_op jit(solution)/shard_map/ppermute | solution.py:34
  20.1 0.0 collective-permute-done.12.rest_4_
  20.1 0.8 %collective-permute-done.7.rest_5_ = bf16[528,128]{1,0:T(8,128)(2,1)S(1)} collective-permute-done((bf16[528,128]{1,0:T(8,128)(2,1)S(1)}, bf16[528,128]{1,0:T(8,128)(2,1)S(1)}, u32[]{:S(2)}, u32[]{:S(2)}) %collective-permute-start.7) | collective-permute-done | bytes 135200 | tf_op jit(solution)/shard_map/ppermute | solution.py:34
  20.9 1.5 %collective-permute-start.13 = (bf16[528,128]{1,0:T(8,128)(2,1)S(1)}, bf16[528,128]{1,0:T(8,128)(2,1)S(1)}, u32[]{:S(2)}, u32[]{:S(2)}) collective-permute-start(bf16[528,128]{1,0:T(8,128)(2,1)S(1)} %collective-permute-done.12.rest_4_), channel_id=1, source_target_pairs={{0,16},{16,0},{1,17},{17,1},{2,18},{18,2},{3,19},{19,3},{4,20},{20... | collective-permute-start | bytes 405512 | tf_op jit(solution)/shard_map/ppermute | solution.py:34
  22.4 1.1 %collective-permute-done.10.rest_3_ = bf16[528,128]{1,0:T(8,128)(2,1)S(1)} collective-permute-done((bf16[528,128]{1,0:T(8,128)(2,1)S(1)}, bf16[528,128]{1,0:T(8,128)(2,1)S(1)}, u32[]{:S(2)}, u32[]{:S(2)}) %collective-permute-start.10) | collective-permute-done | bytes 135200 | tf_op jit(solution)/shard_map/ppermute | solution.py:34
  23.5 1.4 %collective-permute-start.11 = (bf16[528,128]{1,0:T(8,128)(2,1)S(1)}, bf16[528,128]{1,0:T(8,128)(2,1)S(1)}, u32[]{:S(2)}, u32[]{:S(2)}) collective-permute-start(bf16[528,128]{1,0:T(8,128)(2,1)S(1)} %collective-permute-done.10.rest_3_), channel_id=1, source_target_pairs={{0,16},{16,0},{1,17},{17,1},{2,18},{18,2},{3,19},{19,3},{4,20},{20... | collective-permute-start | bytes 405512 | tf_op jit(solution)/shard_map/ppermute | solution.py:34
  24.9 0.0 collective-permute-start.4
  24.9 2.4 %collective-permute-done.5.rest_3_ = bf16[256,128]{1,0:T(8,128)(2,1)S(1)} collective-permute-done((bf16[256,128]{1,0:T(8,128)(2,1)S(1)}, bf16[256,128]{1,0:T(8,128)(2,1)S(1)}, u32[]{:S(2)}, u32[]{:S(2)}) %collective-permute-start.5) | collective-permute-done | bytes 65568 | tf_op jit(solution)/shard_map/ppermute | solution.py:34
  27.3 0.0 collective-permute-done.6.rest_4_
  27.3 1.5 %collective-permute-start.9 = (bf16[272,128]{1,0:T(8,128)(2,1)S(1)}, bf16[272,128]{1,0:T(8,128)(2,1)S(1)}, u32[]{:S(2)}, u32[]{:S(2)}) collective-permute-start(bf16[272,128]{1,0:T(8,128)(2,1)S(1)} %collective-permute-done.6.rest_4_), channel_id=1, source_target_pairs={{0,16},{16,0},{1,17},{17,1},{2,18},{18,2},{3,19},{19,3},{4,20},{20... | collective-permute-start | bytes 208904 | tf_op jit(solution)/shard_map/ppermute | solution.py:34
  28.8 0.5 %collective-permute-start.8 = (bf16[256,128]{1,0:T(8,128)(2,1)S(1)}, bf16[256,128]{1,0:T(8,128)(2,1)S(1)}, u32[]{:S(2)}, u32[]{:S(2)}) collective-permute-start(bf16[256,128]{1,0:T(8,128)(2,1)S(1)} %collective-permute-done.5.rest_3_), channel_id=1, source_target_pairs={{0,16},{16,0},{1,17},{17,1},{2,18},{18,2},{3,19},{19,3},{4,20},{20... | collective-permute-start | bytes 196616 | tf_op jit(solution)/shard_map/ppermute | solution.py:34
  29.3 0.0 collective-permute-done.4.rest_2_
  29.3 0.0 collective-permute-done.13.rest_6_
  29.3 0.6 %product.3.rest_5_ = f32[256,512]{1,0:T(8,128)S(1)} custom-call(f32[8,128]{1,0:T(8,128)S(1)} %get-tuple-element.27.goals, bf16[4,256,128]{2,1,0:T(8,128)(2,1)S(1)} %get-tuple-element.29.rest_0_, bf16[2,256,128]{2,1,0:T(8,128)(2,1)S(1)} %collective-permute-done.3.rest_1_, bf16[2,256,128]{2,1,0:T(8,128)(2,1)S(1)} %collective-permute-done.4.rest_2_, ...), custom_call_target="tpu_custom_call" | custom-call | tf_op jit(solution)/shard_map/product/pallas_call | solution.py:268
  29.9 0.0 collective-permute-done.11.rest_4_
  30.0 0.4 %product.4.rest_7_ = f32[256,512]{1,0:T(8,128)S(1)} custom-call(f32[8,128]{1,0:T(8,128)S(1)} %get-tuple-element.27.goals, bf16[4,256,128]{2,1,0:T(8,128)(2,1)S(1)} %get-tuple-element.29.rest_0_, bf16[2,256,128]{2,1,0:T(8,128)(2,1)S(1)} %collective-permute-done.3.rest_1_, bf16[2,256,128]{2,1,0:T(8,128)(2,1)S(1)} %collective-permute-done.4.rest_2_, ...), custom_call_target="tpu_custom_call" | custom-call | tf_op jit(solution)/shard_map/product/pallas_call | solution.py:268
  30.4 2.7 %collective-permute-done.8.rest_5_ = bf16[256,128]{1,0:T(8,128)(2,1)S(1)} collective-permute-done((bf16[256,128]{1,0:T(8,128)(2,1)S(1)}, bf16[256,128]{1,0:T(8,128)(2,1)S(1)}, u32[]{:S(2)}, u32[]{:S(2)}) %collective-permute-start.8) | collective-permute-done | bytes 65568 | tf_op jit(solution)/shard_map/ppermute | solution.py:34
  33.1 0.0 collective-permute-done.9.rest_6_
  33.1 1.1 %product.5 = bf16[1024,128]{1,0:T(8,128)(2,1)} custom-call(f32[8,128]{1,0:T(8,128)S(1)} %get-tuple-element.27.goals, bf16[4,256,128]{2,1,0:T(8,128)(2,1)S(1)} %get-tuple-element.29.rest_0_, bf16[2,256,128]{2,1,0:T(8,128)(2,1)S(1)} %collective-permute-done.3.rest_1_, bf16[2,256,128]{2,1,0:T(8,128)(2,1)S(1)} %collective-permute-done.4.rest_2_, ...), custom_call_target="tpu_custom_call" | custom-call | tf_op jit(solution)/shard_map/product/pallas_call | solution.py:268
Async XLA Ops:
  1.2 3.2 %collective-permute-start = (bf16[528,128]{1,0:T(8,128)(2,1)S(1)}, bf16[528,128]{1,0:T(8,128)(2,1)S(1)}, u32[]{:S(2)}, u32[]{:S(2)}) collective-permute-start(bf16[528,128]{1,0:T(8,128)(2,1)S(1)} %get-tuple-element.28), channel_id=1, source_target_pairs={{0,1},{1,0},{2,3},{3,2},{4,5},{5,4},{6,7},{7,6},{8,9},{9,8},{10,11... | collective-permute-start | bytes 405512 | tf_op jit(solution)/shard_map/ppermute | solution.py:34
  1.7 7.0 %collective-permute-start.1 = (bf16[528,128]{1,0:T(8,128)(2,1)S(1)}, bf16[528,128]{1,0:T(8,128)(2,1)S(1)}, u32[]{:S(2)}, u32[]{:S(2)}) collective-permute-start(bf16[528,128]{1,0:T(8,128)(2,1)S(1)} %get-tuple-element.31), channel_id=1, source_target_pairs={{0,2},{1,3},{2,0},{3,1},{4,6},{5,7},{6,4},{7,5},{8,10},{9,11},{10,... | collective-permute-start | bytes 405512 | tf_op jit(solution)/shard_map/ppermute | solution.py:34
  4.3 6.8 %collective-permute-start.2 = (bf16[528,128]{1,0:T(8,128)(2,1)S(1)}, bf16[528,128]{1,0:T(8,128)(2,1)S(1)}, u32[]{:S(2)}, u32[]{:S(2)}) collective-permute-start(bf16[528,128]{1,0:T(8,128)(2,1)S(1)} %get-tuple-element.32), channel_id=1, source_target_pairs={{0,3},{1,2},{2,1},{3,0},{4,7},{5,6},{6,5},{7,4},{8,11},{9,10},{10,... | collective-permute-start | bytes 405512 | tf_op jit(solution)/shard_map/ppermute | solution.py:34
  5.6 5.8 %collective-permute-start.3 = (bf16[2,256,128]{2,1,0:T(8,128)(2,1)S(1)}, bf16[2,256,128]{2,1,0:T(8,128)(2,1)S(1)}, u32[]{:S(2)}, u32[]{:S(2)}) collective-permute-start(bf16[2,256,128]{2,1,0:T(8,128)(2,1)S(1)} %get-tuple-element.33), channel_id=1, source_target_pairs={{0,16},{16,0},{1,17},{17,1},{2,18},{18,2},{3,19},{19,3},{4,20},{20... | collective-permute-start | bytes 393224 | tf_op jit(solution)/shard_map/ppermute | solution.py:34
  11.7 8.3 %collective-permute-start.12 = (bf16[528,128]{1,0:T(8,128)(2,1)S(1)}, bf16[528,128]{1,0:T(8,128)(2,1)S(1)}, u32[]{:S(2)}, u32[]{:S(2)}) collective-permute-start(bf16[528,128]{1,0:T(8,128)(2,1)S(1)} %get-tuple-element.47), channel_id=1, source_target_pairs={{0,12},{4,8},{8,4},{12,0},{1,13},{5,9},{9,5},{13,1},{2,14},{6,10},... | collective-permute-start | bytes 405512 | tf_op jit(solution)/shard_map/ppermute | solution.py:34
  15.6 5.3 %collective-permute-start.7 = (bf16[528,128]{1,0:T(8,128)(2,1)S(1)}, bf16[528,128]{1,0:T(8,128)(2,1)S(1)}, u32[]{:S(2)}, u32[]{:S(2)}) collective-permute-start(bf16[528,128]{1,0:T(8,128)(2,1)S(1)} %get-tuple-element.42.rest_3_), channel_id=1, source_target_pairs={{0,16},{16,0},{1,17},{17,1},{2,18},{18,2},{3,19},{19,3},{4,20},{20... | collective-permute-start | bytes 405512 | tf_op jit(solution)/shard_map/ppermute | solution.py:34
  17.1 6.4 %collective-permute-start.10 = (bf16[528,128]{1,0:T(8,128)(2,1)S(1)}, bf16[528,128]{1,0:T(8,128)(2,1)S(1)}, u32[]{:S(2)}, u32[]{:S(2)}) collective-permute-start(bf16[528,128]{1,0:T(8,128)(2,1)S(1)} %get-tuple-element.45), channel_id=1, source_target_pairs={{0,4},{4,0},{8,12},{12,8},{1,5},{5,1},{9,13},{13,9},{2,6},{6,2},{1... | collective-permute-start | bytes 405512 | tf_op jit(solution)/shard_map/ppermute | solution.py:34
  17.1 10.2 %collective-permute-start.6 = (bf16[272,128]{1,0:T(8,128)(2,1)S(1)}, bf16[272,128]{1,0:T(8,128)(2,1)S(1)}, u32[]{:S(2)}, u32[]{:S(2)}) collective-permute-start(bf16[272,128]{1,0:T(8,128)(2,1)S(1)} %get-tuple-element.41), channel_id=1, source_target_pairs={{0,8},{4,12},{8,0},{12,4},{1,9},{5,13},{9,1},{13,5},{2,10},{6,14},... | collective-permute-start | bytes 208904 | tf_op jit(solution)/shard_map/ppermute | solution.py:34
  17.9 9.4 %collective-permute-start.5 = (bf16[256,128]{1,0:T(8,128)(2,1)S(1)}, bf16[256,128]{1,0:T(8,128)(2,1)S(1)}, u32[]{:S(2)}, u32[]{:S(2)}) collective-permute-start(bf16[256,128]{1,0:T(8,128)(2,1)S(1)} %get-tuple-element.40), channel_id=1, source_target_pairs={{0,8},{4,12},{8,0},{12,4},{1,9},{5,13},{9,1},{13,5},{2,10},{6,14},... | collective-permute-start | bytes 196616 | tf_op jit(solution)/shard_map/ppermute | solution.py:34
  20.9 8.4 %collective-permute-start.13 = (bf16[528,128]{1,0:T(8,128)(2,1)S(1)}, bf16[528,128]{1,0:T(8,128)(2,1)S(1)}, u32[]{:S(2)}, u32[]{:S(2)}) collective-permute-start(bf16[528,128]{1,0:T(8,128)(2,1)S(1)} %collective-permute-done.12.rest_4_), channel_id=1, source_target_pairs={{0,16},{16,0},{1,17},{17,1},{2,18},{18,2},{3,19},{19,3},{4,20},{20... | collective-permute-start | bytes 405512 | tf_op jit(solution)/shard_map/ppermute | solution.py:34
  23.5 6.4 %collective-permute-start.11 = (bf16[528,128]{1,0:T(8,128)(2,1)S(1)}, bf16[528,128]{1,0:T(8,128)(2,1)S(1)}, u32[]{:S(2)}, u32[]{:S(2)}) collective-permute-start(bf16[528,128]{1,0:T(8,128)(2,1)S(1)} %collective-permute-done.10.rest_3_), channel_id=1, source_target_pairs={{0,16},{16,0},{1,17},{17,1},{2,18},{18,2},{3,19},{19,3},{4,20},{20... | collective-permute-start | bytes 405512 | tf_op jit(solution)/shard_map/ppermute | solution.py:34
  24.9 4.4 %collective-permute-start.4 = (bf16[2,256,128]{2,1,0:T(8,128)(2,1)S(1)}, bf16[2,256,128]{2,1,0:T(8,128)(2,1)S(1)}, u32[]{:S(2)}, u32[]{:S(2)}) collective-permute-start(bf16[2,256,128]{2,1,0:T(8,128)(2,1)S(1)} %collective-permute-done.3.rest_1_), channel_id=1, source_target_pairs={{0,1},{1,0},{2,3},{3,2},{4,5},{5,4},{6,7},{7,6},{8,9},{9,8},{10,11... | collective-permute-start | bytes 393224 | tf_op jit(solution)/shard_map/ppermute | solution.py:34
  27.3 5.8 %collective-permute-start.9 = (bf16[272,128]{1,0:T(8,128)(2,1)S(1)}, bf16[272,128]{1,0:T(8,128)(2,1)S(1)}, u32[]{:S(2)}, u32[]{:S(2)}) collective-permute-start(bf16[272,128]{1,0:T(8,128)(2,1)S(1)} %collective-permute-done.6.rest_4_), channel_id=1, source_target_pairs={{0,16},{16,0},{1,17},{17,1},{2,18},{18,2},{3,19},{19,3},{4,20},{20... | collective-permute-start | bytes 208904 | tf_op jit(solution)/shard_map/ppermute | solution.py:34
  28.8 4.3 %collective-permute-start.8 = (bf16[256,128]{1,0:T(8,128)(2,1)S(1)}, bf16[256,128]{1,0:T(8,128)(2,1)S(1)}, u32[]{:S(2)}, u32[]{:S(2)}) collective-permute-start(bf16[256,128]{1,0:T(8,128)(2,1)S(1)} %collective-permute-done.5.rest_3_), channel_id=1, source_target_pairs={{0,16},{16,0},{1,17},{17,1},{2,18},{18,2},{3,19},{19,3},{4,20},{20... | collective-permute-start | bytes 196616 | tf_op jit(solution)/shard_map/ppermute | solution.py:34

commit v3 on v2

v3 whole, which is shorter than its diff:
```python
import functools

import jax
import jax.numpy as jnp
from jax import lax
from jax.experimental import pallas as pl
from jax.experimental.pallas import tpu as pltpu
from jax.sharding import PartitionSpec as P

WHOLE = 2
DIGIT = 8
VMEM = pl.BlockSpec(memory_space=pltpu.VMEM)
SMEM = pl.BlockSpec(memory_space=pltpu.SMEM)
HBM = pl.BlockSpec(memory_space=pltpu.HBM)
SMALL = pltpu.CompilerParams(vmem_limit_bytes=8 * 1024 * 1024)


def mate(index, step, size):
    return index ^ step if size & (size - 1) == 0 else (index - step) % size


def target(index, step, size):
    return index ^ step if size & (size - 1) == 0 else (index + step) % size


def round_of(index, source, size):
    return index ^ source if size & (size - 1) == 0 else lax.rem(index - source + size, size)


def exchange(block, axis, step, size, stride=1):
    route = []
    for place in range(size * stride):
        high, low = divmod(place, stride)
        route.append((place, target(high, step, size) * stride + low))
    return lax.ppermute(block, axis, route)


def id_rows(stored):
    return -(-4 * stored // 16) * 16


def rows_of(span, stored, side):
    return (span[1] - span[0]) * side + (id_rows(stored) if span[1] == 2 * stored else 0)


def find(pieces, spans, block, side):
    for piece, (low, high) in zip(pieces, spans):
        if low <= block < high:
            return piece, (block - low) * side


def pack_kernel(stride, spans, x_far, x2_far, *rest):
    groups, stored, side = x_far.shape[1:4]
    fars, rest = rest[:4], list(rest[4:])
    outs = [[rest.pop(0) for _ in cut] for cut in spans]
    (choice, goals), nears, (sems, id_sems) = rest[:2], rest[2:-2], rest[-2:]
    cols_ref, cols2_ref, wanted_ref, goals_ref = nears
    count = id_rows(stored)
    own = lax.axis_index("col")
    ids = [
        pltpu.make_async_copy(far, near, id_sems.at[at]) for at, (far, near) in enumerate(zip(fars, nears))
    ]
    loads = []
    for step, out in enumerate(outs):
        reader = target(own, step, groups)
        for block in range(2 * stored):
            piece, first = find(out, spans[step], block, side)
            far = (x_far, x2_far)[block // stored].at[0, reader, block % stored]
            loads.append(pltpu.make_async_copy(far, piece.at[pl.ds(first, side)], sems.at[step, block]))
    for load in ids + loads:
        load.start()
    for load in ids:
        load.wait()
    row = lax.broadcasted_iota(jnp.int32, (count, side), 0)
    for step, out in enumerate(outs):
        reader = target(own, step, groups)
        digits = jnp.zeros((count, side), jnp.int32)
        for block in range(2 * stored):
            value = (cols_ref, cols2_ref)[block // stored][0, block % stored, reader]
            digits = jnp.where(row == 2 * block, value >> DIGIT, digits)
            digits = jnp.where(row == 2 * block + 1, value & ((1 << DIGIT) - 1), digits)
        first = out[-1].shape[0] - count
        out[-1][pl.ds(first, count), :] = digits.astype(jnp.float32).astype(out[-1].dtype)
    own_row = lax.axis_index("row")
    high, low = own_row // stride, own_row % stride
    row = lax.broadcasted_iota(jnp.int32, choice.shape, 0)
    came = jnp.zeros(choice.shape, jnp.int32)
    for step in range(groups):
        reader = target(high, step, groups)
        slot = lax.rem(high - reader + groups, groups)
        owner = lax.rem(wanted_ref[0, reader * stride + low, slot], groups)
        came = jnp.where(row // groups == step, round_of(own, owner, groups), came)
    choice[...] = jnp.where(row % groups == came, 1.0, 0.0)
    row = lax.broadcasted_iota(jnp.int32, goals.shape, 0)
    goal = jnp.zeros(goals.shape, jnp.int32)
    for s in range(goals_ref.shape[2]):
        goal = jnp.where(row == s, goals_ref[0, 0, s], goal)
    goals[...] = goal.astype(jnp.float32)
    for load in loads:
        load.wait()


def pinned(array):
    return pltpu.with_memory_space_constraint(array, pltpu.HBM)


def pack(x_tiles, x2_tiles, x_cols, x2_cols, requests, out_cols, stride, spans):
    _, groups, stored, side, _ = x_tiles.shape
    kind = x_tiles.dtype
    small = (jnp.swapaxes(x_cols, 1, 2), jnp.swapaxes(x2_cols, 1, 2), requests, out_cols)
    shapes = [jax.ShapeDtypeStruct((rows_of(span, stored, side), side), kind) for cut in spans for span in cut]
    shapes += [
        jax.ShapeDtypeStruct((groups * groups, side), jnp.float32),
        jax.ShapeDtypeStruct((-(-out_cols.shape[2] // 8) * 8, side), jnp.float32),
    ]
    out = pl.pallas_call(
        functools.partial(pack_kernel, stride, spans),
        out_shape=shapes,
        in_specs=[HBM] * 6,
        out_specs=[VMEM] * len(shapes),
        scratch_shapes=[pltpu.SMEM(array.shape, array.dtype) for array in small]
        + [pltpu.SemaphoreType.DMA((groups, 2 * stored)), pltpu.SemaphoreType.DMA((len(small),))],
        compiler_params=SMALL,
        name="pack",
    )(pinned(x_tiles), pinned(x2_tiles), *map(pinned, small))
    flat = iter(out)
    return [[next(flat) for _ in cut] for cut in spans], *flat


def split_kernel(slots, slab_far, _, own_ref, *rest):
    outs, (wide, slab_ref, sems) = rest[:-3], rest[-3:]
    layers, pieces = len(outs) + 1, sems.shape[0]
    rows = slab_far.shape[0] // layers
    share = rows // pieces
    own, parity = lax.axis_index("layer"), lax.axis_index("col") % 2
    firsts = [target(own, step, layers) * rows for step in range(layers)]
    loads = [
        [
            pltpu.make_async_copy(
                slab_far.at[pl.ds(pl.multiple_of(first + at * share, share), share)],
                slab_ref.at[step, pl.ds(at * share, share)],
                sems.at[at, step],
            )
            for at in range(pieces)
        ]
        for step, first in enumerate(firsts)
    ]
    for load in sum(loads, []):
        load.start()
    for step in reversed(range(layers)):
        for load in loads[step]:
            load.wait()
        wide[...] = slab_ref[step].astype(jnp.float32)
        if step:
            half = slots // 2
            for slot in range(half):
                picked = wide[pl.ds(parity * half + slot, rows // slots, stride=slots)]
                outs[step - 1][slot] = picked.astype(own_ref.dtype)
        else:
            for slot in range(slots):
                own_ref[slot] = wide[pl.ds(slot, rows // slots, stride=slots)].astype(own_ref.dtype)


def split(slab_tiles, after, layers):
    high, per, _, slots, side = slab_tiles.shape
    rows = high * per // layers
    kind = slab_tiles.dtype
    out = pl.pallas_call(
        functools.partial(split_kernel, slots),
        out_shape=[jax.ShapeDtypeStruct((slots, rows, side), kind)]
        + [jax.ShapeDtypeStruct((slots // 2, rows, side), kind)] * (layers - 1),
        in_specs=[HBM, pl.BlockSpec(memory_space=pl.ANY)],
        out_specs=[VMEM] * layers,
        scratch_shapes=[
            pltpu.VMEM((rows * slots, side), jnp.float32),
            pltpu.VMEM((layers, rows * slots, side), kind),
            pltpu.SemaphoreType.DMA((4, layers)),
        ],
        compiler_params=SMALL,
        name="split",
    )(pinned(slab_tiles.reshape(high * per * slots, side)), after)
    return out[0], list(out[1:])


def pick_kernel(spans, wanted, stored, choice, *rest):
    held, outs = list(rest[: -len(wanted)]), rest[-len(wanted) :]
    held = [[held.pop(0) for _ in cut] for cut in spans]
    groups, side = len(held), choice.shape[1]
    count = id_rows(stored)
    for out, (step, span) in zip(outs, wanted):
        hits = [
            jnp.broadcast_to(choice[step * groups + at : step * groups + at + 1, :], (side, side)).astype(out.dtype)
            for at in range(groups)
        ]
        for block in range(*span):
            total = jnp.zeros((side, side), out.dtype)
            for at in range(groups):
                piece, first = find(held[at], spans[at], block, side)
                total += piece[pl.ds(first, side), :] * hits[at]
            out[pl.ds((block - span[0]) * side, side), :] = total
        if span[1] == 2 * stored:
            total = jnp.zeros((count, side), out.dtype)
            for at in range(groups):
                total += held[at][-1][pl.ds(held[at][-1].shape[0] - count, count), :] * hits[at][:count]
            out[pl.ds(out.shape[0] - count, count), :] = total


def pick(choice, held, spans, wanted, stored):
    side, kind = held[0][0].shape[1], held[0][0].dtype
    flat = [piece for block in held for piece in block]
    return pl.pallas_call(
        functools.partial(pick_kernel, spans, wanted, stored),
        out_shape=[jax.ShapeDtypeStruct((rows_of(span, stored, side), side), kind) for _, span in wanted],
        in_specs=[VMEM] * (1 + len(flat)),
        out_specs=[VMEM] * len(wanted),
        compiler_params=SMALL,
        name="pick",
    )(choice, *flat)


def product_kernel(stride, groups, layers, stored, items, wanted, last, goals, *rest):
    lefts, rest = rest[: 2 * layers - 1], list(rest[2 * layers - 1 :])
    slots, rows, side = lefts[0].shape
    half = slots // 2
    high, parity = lax.axis_index("row") // stride, lax.axis_index("col") % 2
    left_parts, sums = ([], []), ([], [])
    for layer in range(layers):
        for step, spans in items:
            slot = lax.rem(mate(high, step, groups) - high + groups, groups)
            if layer:
                same, other = lefts[2 * layer - 1], lefts[2 * layer]
                at = lax.rem(slot, half)
                left = jnp.where(slot // half == parity, same[at], other[at])
            else:
                left = lefts[0][slot]
            ids = rest.pop(0)
            digits = ids[pl.ds(ids.shape[0] - id_rows(stored), id_rows(stored)), :].astype(jnp.float32)
            pieces = [ids if span[1] == 2 * stored else rest.pop(0) for span in spans]
            for part in range(2):
                blocks = [b for low, high_ in spans for b in range(low, high_) if b // stored == part]
                if not blocks:
                    continue
                across = [jnp.zeros((side, side), jnp.bfloat16)] * wanted
                for block in blocks:
                    piece, first = find(pieces, spans, block, side)
                    tile = piece[pl.ds(first, side), :]
                    listed = (
                        digits[2 * block : 2 * block + 1] * (1 << DIGIT)
                        + digits[2 * block + 1 : 2 * block + 2]
                    )
                    for s in range(wanted):
                        hit = jnp.where(listed == goals[s : s + 1, :], 1.0, 0.0)
                        hit = jnp.broadcast_to(hit, (side, side))
                        across[s] = across[s] + tile * hit.astype(jnp.bfloat16)
                sums[part].append(jnp.concatenate(across, axis=1))
                left_parts[part].append(left)
    summed = None
    for factor, left, chosen in zip((4.0, -3.0), left_parts, sums):
        if left:
            term = factor * jnp.dot(
                jnp.concatenate(left, axis=1),
                jnp.concatenate(chosen, axis=0),
                preferred_element_type=jnp.float32,
            )
            summed = term if summed is None else summed + term
    if last:
        tall = rest.pop()
    out_ref = rest.pop()
    if rest:
        summed += rest.pop()[...]
    if last:
        for s in range(wanted):
            tall[pl.ds(s, rows, stride=wanted)] = summed[:, s * side : (s + 1) * side]
        summed = tall[...]
    out_ref[...] = summed.astype(out_ref.dtype)


def product(lefts, blocks, total, goals, wanted, stored, stride, items, last):
    layers, groups = len(blocks), len(blocks[0])
    _, rows, side = lefts[0].shape
    flat = []
    for of_layer in blocks:
        for step, spans in items:
            flat.append(of_layer[step][max(of_layer[step])])
            flat += [of_layer[step][span] for span in spans if span[1] < 2 * stored]
    flat += [] if total is None else [total]
    shape = (rows * wanted, side) if last else (rows, wanted * side)
    return pl.pallas_call(
        functools.partial(product_kernel, stride, groups, layers, stored, items, wanted, last),
        out_shape=jax.ShapeDtypeStruct(shape, lefts[0].dtype if last else jnp.float32),
        in_specs=[VMEM] * (1 + len(lefts) + len(flat)),
        out_specs=VMEM,
        scratch_shapes=[pltpu.VMEM(shape, jnp.float32)] if last else [],
        compiler_params=pltpu.CompilerParams(vmem_limit_bytes=16 * 1024 * 1024),
        name="product",
    )(goals, *lefts, *flat)


def body(slab_tiles, x_tiles, x_cols, x2_tiles, x2_cols, requests, out_cols):
    layers, rows, groups = (lax.axis_size(axis) for axis in ("layer", "row", "col"))
    stride = rows // groups
    _, _, stored, side, _ = x_tiles.shape
    all_blocks = (0, 2 * stored)
    col_cut, G = [all_blocks], {'seq': [('A',), ('pick', 0), ('z', 'far', 0), ('z', 'near', 0), ('z', 'last', 0), ('x', 'own', 0), ('x', 'far', 0), ('x', 'last', 0), ('x', 'near', 0)], 'split': ('y', 'near', 0), 'stages': [['far'], ['own', 'near'], ['last']], ('pick', 0): (('A',),), ('x', 'far', 0): (('x', 'own', 0),), ('x', 'near', 0): (('x', 'own', 0),), ('x', 'last', 0): (('x', 'own', 0),)}
    far = list(reversed(range(WHOLE, groups)))
    spans = [[all_blocks] if k < WHOLE else col_cut for k in range(groups)]
    row_cut = [[all_blocks] if k in far[:-1] else [all_blocks] if k >= WHOLE else [[all_blocks], [all_blocks]][k == 0] for k in range(groups)]
    done = {}

    def gated(value, names):
        after = [done[name] for name in names if name in done]
        return lax.optimization_barrier((value, after))[0] if after else value

    def label(k):
        return "own" if k == 0 else "near" if k < WHOLE else "far" if k != far[-1] else "last"

    packed, choice, goals = pack(x_tiles, x2_tiles, x_cols, x2_cols, requests, out_cols, stride, spans)
    held = [packed[0]] + [[exchange(piece, "col", k, groups) for piece in packed[k]] for k in range(1, groups)]
    for k in range(1, groups):
        for part, piece in enumerate(held[k]):
            done["y", label(k), part] = piece
    got = [{} for _ in range(groups)]
    blocks = [got] + [[{} for _ in range(groups)] for _ in range(1, layers)]

    def row(k, span, piece):
        name = ("z", label(k), row_cut[k].index(span))
        got[k][span] = done[name] = exchange(gated(piece, G.get(name, ())), "row", k, groups, stride)

    def forward(k, span):
        name = ("x", label(k), row_cut[k].index(span))
        piece = gated(got[k][span], G.get(name, ()))
        for step in range(1, layers):
            blocks[step][k][span] = done[name] = exchange(piece, "layer", step, layers)

    def slab():
        own, sent = split(slab_tiles, done[G["split"]], layers)
        sent = [exchange(gated(sent[k - 1], G.get(("A",), ())), "layer", k, layers) for k in range(1, layers)]
        done["A",] = sent[0]
        return [own] + [left for same in sent for left in (same, exchange(same, "col", 1, groups))]

    def choose(stage):
        low, high = col_cut[stage]
        wanted = [(k, span) for k in range(WHOLE) for span in row_cut[k] if stage == len(col_cut) - 1]
        wanted += [(k, span) for k in far for span in row_cut[k] if low < span[1] <= high]
        ready = [block if k < WHOLE else block[: stage + 1] for k, block in enumerate(held)]
        ready = gated(ready, G.get(("pick", stage), ()))
        here = [cut[: len(block)] for cut, block in zip(spans, ready)]
        picked = pick(choice, ready, here, wanted, stored)
        done["pick", stage] = picked[0]
        for (k, span), piece in zip(wanted, picked):
            chosen[k, span] = piece

    chosen, lefts = {}, None
    for token in G["seq"]:
        if token[0] == "pick":
            choose(token[1])
        elif token[0] == "A":
            lefts = slab()
        else:
            rounds = {"own": [0], "near": list(range(1, WHOLE)), "far": far[:-1], "last": far[-1:]}[token[1]]
            for k in rounds:
                span = row_cut[k][token[2]]
                if k == 0:
                    got[0][span] = chosen[0, span]
                if token[0] == "z":
                    row(k, span, chosen[k, span])
                else:
                    forward(k, span)

    def add(total, items, last):
        return product(lefts, blocks, total, goals, out_cols.shape[2], stored, stride, items, last)

    total = None
    for stage in G["stages"]:
        rounds = {"own": [0], "near": list(range(1, WHOLE)), "far": far[:-1], "last": far[-1:]}
        items = [(k, tuple(row_cut[k])) for name in stage for k in rounds[name]]
        total = add(total, items, stage is G["stages"][-1])
    high, per = slab_tiles.shape[0] // layers, slab_tiles.shape[1]
    return total.reshape(high, per, 1, out_cols.shape[2], side)


def solution(mesh):
    placed = (
        P(None, "row", "layer", None, None),
        P(("layer", "row", "col"), None, None, None, None),
        P(("layer", "row", "col"), None, None),
        P(("layer", "row", "col"), None, None, None, None),
        P(("layer", "row", "col"), None, None),
        P("layer", None, None),
        P("row", "col", None),
    )
    return jax.shard_map(
        body,
        mesh=mesh,
        in_specs=placed,
        out_specs=P("layer", "row", "col", None, None),
        check_vma=False,
    )
```

time: 34.5 us -> 33.7 us (0.977)
  starting transfers between devices: 18.2 us -> 15.5 us
  waiting for transfers between devices: 11.1 us -> 13 us
    ppermute x14 -> x12, starting transfers between devices: 18.2 us -> 15.5 us  [exchange(): return lax.ppermute(block, axis, route)]
    ppermute x14 -> x12, waiting for transfers between devices: 11.1 us -> 13 us  [exchange(): return lax.ppermute(block, axis, route)]
  transfers between devices with their start and end apart: 14 -> 12, of which waited for: 7 -> 9; matrix products, arithmetic and copies ran while one was open for 0% -> 0% of each run, Pallas kernels for 7% -> 7%
where the time goes in v3:
time: 33.7 us; the launch traced here: 33.4 us
  starting transfers between devices  15.5 us (46%)
  waiting for transfers between devices  13 us (39%)
  Pallas kernels  4.87 us (14%)
    ppermute x12, starting transfers between devices, exchange(): return lax.ppermute(block, axis, route)  15.5 us
    ppermute x12, waiting for transfers between devices, exchange(): return lax.ppermute(block, axis, route)  13 us
    pallas_call x3, Pallas kernels, product(): pl.pallas_call(functools.partial(product_kernel, stride, groups, layers,...  2.13 us
    pallas_call x1, Pallas kernels, split(): pl.pallas_call(functools.partial(split_kernel, slots), out_shape=[jax.Sha...  1.27 us
    pallas_call x1, Pallas kernels, pack(): pl.pallas_call(functools.partial(pack_kernel, stride, spans), out_shape=s...  1.17 us
  transfers between devices with their start and end apart: 12, of which 9 were waited for; matrix products, arithmetic and copies ran while one was open for 0% of the time, Pallas kernels for 7%

profile of v3, /device:TPU:0, one launch (start us, length us, event | category | flops | bytes accessed | tf_op | source)
XLA Modules:
  0.0 33.4 jit_solution(6678123514813186930)
XLA Ops:
  0.0 1.2 %pack.1 = (bf16[528,128]{1,0:T(8,128)(2,1)S(1)}, bf16[528,128]{1,0:T(8,128)(2,1)S(1)}, bf16[528,128]{1,0:T(8,128)(2,1)S(1)}, bf16[528,128]{1,0:T(8,128)(2,1)S(1)...) custom-call(bf16[1,4,2,128,128]{4,3,2,1,0:T(8,128)(2,1)} %x_far.1, bf16[1,4,2,128,128]{4,3,2,1,0:T(8,128)(2,1)} %x2_far.1, ...), custom_call_target="tpu_custom_call" | custom-call | tf_op jit(solution)/shard_map/pack/pallas_call | solution.py:116
  1.2 0.5 %collective-permute-start = (bf16[528,128]{1,0:T(8,128)(2,1)S(1)}, bf16[528,128]{1,0:T(8,128)(2,1)S(1)}, u32[]{:S(2)}, u32[]{:S(2)}) collective-permute-start(bf16[528,128]{1,0:T(8,128)(2,1)S(1)} %get-tuple-element.25), channel_id=1, source_target_pairs={{0,1},{1,0},{2,3},{3,2},{4,5},{5,4},{6,7},{7,6},{8,9},{9,8},{10,11... | collective-permute-start | bytes 405512 | tf_op jit(solution)/shard_map/ppermute | solution.py:35
  1.7 2.6 %collective-permute-start.3 = (bf16[528,128]{1,0:T(8,128)(2,1)S(1)}, bf16[528,128]{1,0:T(8,128)(2,1)S(1)}, u32[]{:S(2)}, u32[]{:S(2)}) collective-permute-start(bf16[528,128]{1,0:T(8,128)(2,1)S(1)} %get-tuple-element.30), channel_id=1, source_target_pairs={{0,2},{1,3},{2,0},{3,1},{4,6},{5,7},{6,4},{7,5},{8,10},{9,11},{10,... | collective-permute-start | bytes 405512 | tf_op jit(solution)/shard_map/ppermute | solution.py:35
  4.3 0.1 collective-permute-start.4
  4.4 0.0 collective-permute-done._.rest_1_
  4.4 1.3 %split.1 = (bf16[4,256,128]{2,1,0:T(8,128)(2,1)S(1)}, bf16[2,256,128]{2,1,0:T(8,128)(2,1)S(1)}) custom-call(bf16[2048,128]{1,0:T(8,128)(2,1)} %bitcast.6, bf16[528,128]{1,0:T(8,128)(2,1)S(1)} %collective-permute-done._.rest_1_), custom_call_target="tpu_custom_call" | custom-call | tf_op jit(solution)/shard_map/split/pallas_call | solution.py:168
  5.6 1.8 %collective-permute-start.1 = (bf16[2,256,128]{2,1,0:T(8,128)(2,1)S(1)}, bf16[2,256,128]{2,1,0:T(8,128)(2,1)S(1)}, u32[]{:S(2)}, u32[]{:S(2)}) collective-permute-start(bf16[2,256,128]{2,1,0:T(8,128)(2,1)S(1)} %get-tuple-element.27), channel_id=1, source_target_pairs={{0,16},{16,0},{1,17},{17,1},{2,18},{18,2},{3,19},{19,3},{4,20},{20... | collective-permute-start | bytes 393224 | tf_op jit(solution)/shard_map/ppermute | solution.py:35
  7.4 1.3 %collective-permute-done.3.rest_2_ = bf16[528,128]{1,0:T(8,128)(2,1)S(1)} collective-permute-done((bf16[528,128]{1,0:T(8,128)(2,1)S(1)}, bf16[528,128]{1,0:T(8,128)(2,1)S(1)}, u32[]{:S(2)}, u32[]{:S(2)}) %collective-permute-start.3) | collective-permute-done | bytes 135200 | tf_op jit(solution)/shard_map/ppermute | solution.py:35
  8.7 2.4 %collective-permute-done.4.rest_3_ = bf16[528,128]{1,0:T(8,128)(2,1)S(1)} collective-permute-done((bf16[528,128]{1,0:T(8,128)(2,1)S(1)}, bf16[528,128]{1,0:T(8,128)(2,1)S(1)}, u32[]{:S(2)}, u32[]{:S(2)}) %collective-permute-start.4) | collective-permute-done | bytes 135200 | tf_op jit(solution)/shard_map/ppermute | solution.py:35
  11.1 0.3 collective-permute-done.1.rest_1_
  11.4 0.3 pick.1
  11.7 3.9 %collective-permute-start.10 = (bf16[528,128]{1,0:T(8,128)(2,1)S(1)}, bf16[528,128]{1,0:T(8,128)(2,1)S(1)}, u32[]{:S(2)}, u32[]{:S(2)}) collective-permute-start(bf16[528,128]{1,0:T(8,128)(2,1)S(1)} %get-tuple-element.41), channel_id=1, source_target_pairs={{0,12},{4,8},{8,4},{12,0},{1,13},{5,9},{9,5},{13,1},{2,14},{6,10},... | collective-permute-start | bytes 405512 | tf_op jit(solution)/shard_map/ppermute | solution.py:35
  15.6 1.5 %collective-permute-start.6 = (bf16[528,128]{1,0:T(8,128)(2,1)S(1)}, bf16[528,128]{1,0:T(8,128)(2,1)S(1)}, u32[]{:S(2)}, u32[]{:S(2)}) collective-permute-start(bf16[528,128]{1,0:T(8,128)(2,1)S(1)} %get-tuple-element.37.rest_3_), channel_id=1, source_target_pairs={{0,16},{16,0},{1,17},{17,1},{2,18},{18,2},{3,19},{19,3},{4,20},{20... | collective-permute-start | bytes 405512 | tf_op jit(solution)/shard_map/ppermute | solution.py:35
  17.1 0.0 collective-permute-start.8
  17.1 0.8 %collective-permute-start.5 = (bf16[528,128]{1,0:T(8,128)(2,1)S(1)}, bf16[528,128]{1,0:T(8,128)(2,1)S(1)}, u32[]{:S(2)}, u32[]{:S(2)}) collective-permute-start(bf16[528,128]{1,0:T(8,128)(2,1)S(1)} %get-tuple-element.36), channel_id=1, source_target_pairs={{0,8},{4,12},{8,0},{12,4},{1,9},{5,13},{9,1},{13,5},{2,10},{6,14},... | collective-permute-start | bytes 405512 | tf_op jit(solution)/shard_map/ppermute | solution.py:35
  17.9 2.1 %collective-permute-done.10.rest_3_ = bf16[528,128]{1,0:T(8,128)(2,1)S(1)} collective-permute-done((bf16[528,128]{1,0:T(8,128)(2,1)S(1)}, bf16[528,128]{1,0:T(8,128)(2,1)S(1)}, u32[]{:S(2)}, u32[]{:S(2)}) %collective-permute-start.10) | collective-permute-done | bytes 135200 | tf_op jit(solution)/shard_map/ppermute | solution.py:35
  20.1 0.8 %collective-permute-done.6.rest_5_ = bf16[528,128]{1,0:T(8,128)(2,1)S(1)} collective-permute-done((bf16[528,128]{1,0:T(8,128)(2,1)S(1)}, bf16[528,128]{1,0:T(8,128)(2,1)S(1)}, u32[]{:S(2)}, u32[]{:S(2)}) %collective-permute-start.6) | collective-permute-done | bytes 135200 | tf_op jit(solution)/shard_map/ppermute | solution.py:35
  20.9 1.5 %collective-permute-start.11 = (bf16[528,128]{1,0:T(8,128)(2,1)S(1)}, bf16[528,128]{1,0:T(8,128)(2,1)S(1)}, u32[]{:S(2)}, u32[]{:S(2)}) collective-permute-start(bf16[528,128]{1,0:T(8,128)(2,1)S(1)} %collective-permute-done.10.rest_3_), channel_id=1, source_target_pairs={{0,16},{16,0},{1,17},{17,1},{2,18},{18,2},{3,19},{19,3},{4,20},{20... | collective-permute-start | bytes 405512 | tf_op jit(solution)/shard_map/ppermute | solution.py:35
  22.4 1.1 %collective-permute-done.8.rest_4_ = bf16[528,128]{1,0:T(8,128)(2,1)S(1)} collective-permute-done((bf16[528,128]{1,0:T(8,128)(2,1)S(1)}, bf16[528,128]{1,0:T(8,128)(2,1)S(1)}, u32[]{:S(2)}, u32[]{:S(2)}) %collective-permute-start.8) | collective-permute-done | bytes 135200 | tf_op jit(solution)/shard_map/ppermute | solution.py:35
  23.5 1.4 %collective-permute-start.9 = (bf16[528,128]{1,0:T(8,128)(2,1)S(1)}, bf16[528,128]{1,0:T(8,128)(2,1)S(1)}, u32[]{:S(2)}, u32[]{:S(2)}) collective-permute-start(bf16[528,128]{1,0:T(8,128)(2,1)S(1)} %collective-permute-done.8.rest_4_), channel_id=1, source_target_pairs={{0,16},{16,0},{1,17},{17,1},{2,18},{18,2},{3,19},{19,3},{4,20},{20... | collective-permute-start | bytes 405512 | tf_op jit(solution)/shard_map/ppermute | solution.py:35
  24.9 2.4 %collective-permute-done.5.rest_3_ = bf16[528,128]{1,0:T(8,128)(2,1)S(1)} collective-permute-done((bf16[528,128]{1,0:T(8,128)(2,1)S(1)}, bf16[528,128]{1,0:T(8,128)(2,1)S(1)}, u32[]{:S(2)}, u32[]{:S(2)}) %collective-permute-start.5) | collective-permute-done | bytes 135200 | tf_op jit(solution)/shard_map/ppermute | solution.py:35
  27.3 1.5 %collective-permute-start.7 = (bf16[528,128]{1,0:T(8,128)(2,1)S(1)}, bf16[528,128]{1,0:T(8,128)(2,1)S(1)}, u32[]{:S(2)}, u32[]{:S(2)}) collective-permute-start(bf16[528,128]{1,0:T(8,128)(2,1)S(1)} %collective-permute-done.5.rest_3_), channel_id=1, source_target_pairs={{0,16},{16,0},{1,17},{17,1},{2,18},{18,2},{3,19},{19,3},{4,20},{20... | collective-permute-start | bytes 405512 | tf_op jit(solution)/shard_map/ppermute | solution.py:35
  28.8 0.0 collective-permute-start.2
  28.8 1.3 %collective-permute-done.2.rest_2_ = bf16[2,256,128]{2,1,0:T(8,128)(2,1)S(1)} collective-permute-done((bf16[2,256,128]{2,1,0:T(8,128)(2,1)S(1)}, bf16[2,256,128]{2,1,0:T(8,128)(2,1)S(1)}, u32[]{:S(2)}, u32[]{:S(2)}) %collective-permute-start.2) | collective-permute-done | bytes 131104 | tf_op jit(solution)/shard_map/ppermute | solution.py:35
  30.1 0.0 collective-permute-done.11.rest_4_
  30.1 0.4 %product.3.rest_7_ = f32[256,512]{1,0:T(8,128)S(1)} custom-call(f32[8,128]{1,0:T(8,128)S(1)} %get-tuple-element.24.goals, bf16[4,256,128]{2,1,0:T(8,128)(2,1)S(1)} %get-tuple-element.26.rest_0_, bf16[2,256,128]{2,1,0:T(8,128)(2,1)S(1)} %collective-permute-done.1.rest_1_, bf16[2,256,128]{2,1,0:T(8,128)(2,1)S(1)} %collective-permute-done.2.rest_2_, ...), custom_call_target="tpu_custom_call" | custom-call | tf_op jit(solution)/shard_map/product/pallas_call | solution.py:288
  30.5 0.0 collective-permute-done.9.rest_6_
  30.5 0.6 %product.4.rest_5_ = f32[256,512]{1,0:T(8,128)S(1)} custom-call(f32[8,128]{1,0:T(8,128)S(1)} %get-tuple-element.24.goals, bf16[4,256,128]{2,1,0:T(8,128)(2,1)S(1)} %get-tuple-element.26.rest_0_, bf16[2,256,128]{2,1,0:T(8,128)(2,1)S(1)} %collective-permute-done.1.rest_1_, bf16[2,256,128]{2,1,0:T(8,128)(2,1)S(1)} %collective-permute-done.2.rest_2_, ...), custom_call_target="tpu_custom_call" | custom-call | tf_op jit(solution)/shard_map/product/pallas_call | solution.py:288
  31.1 1.2 %collective-permute-done.7.rest_4_ = bf16[528,128]{1,0:T(8,128)(2,1)S(1)} collective-permute-done((bf16[528,128]{1,0:T(8,128)(2,1)S(1)}, bf16[528,128]{1,0:T(8,128)(2,1)S(1)}, u32[]{:S(2)}, u32[]{:S(2)}) %collective-permute-start.7) | collective-permute-done | bytes 135200 | tf_op jit(solution)/shard_map/ppermute | solution.py:35
  32.3 1.1 %product.5 = bf16[1024,128]{1,0:T(8,128)(2,1)} custom-call(f32[8,128]{1,0:T(8,128)S(1)} %get-tuple-element.24.goals, bf16[4,256,128]{2,1,0:T(8,128)(2,1)S(1)} %get-tuple-element.26.rest_0_, bf16[2,256,128]{2,1,0:T(8,128)(2,1)S(1)} %collective-permute-done.1.rest_1_, bf16[2,256,128]{2,1,0:T(8,128)(2,1)S(1)} %collective-permute-done.2.rest_2_, ...), custom_call_target="tpu_custom_call" | custom-call | tf_op jit(solution)/shard_map/product/pallas_call | solution.py:288
Async XLA Ops:
  1.2 3.2 %collective-permute-start = (bf16[528,128]{1,0:T(8,128)(2,1)S(1)}, bf16[528,128]{1,0:T(8,128)(2,1)S(1)}, u32[]{:S(2)}, u32[]{:S(2)}) collective-permute-start(bf16[528,128]{1,0:T(8,128)(2,1)S(1)} %get-tuple-element.25), channel_id=1, source_target_pairs={{0,1},{1,0},{2,3},{3,2},{4,5},{5,4},{6,7},{7,6},{8,9},{9,8},{10,11... | collective-permute-start | bytes 405512 | tf_op jit(solution)/shard_map/ppermute | solution.py:35
  1.7 7.0 %collective-permute-start.3 = (bf16[528,128]{1,0:T(8,128)(2,1)S(1)}, bf16[528,128]{1,0:T(8,128)(2,1)S(1)}, u32[]{:S(2)}, u32[]{:S(2)}) collective-permute-start(bf16[528,128]{1,0:T(8,128)(2,1)S(1)} %get-tuple-element.30), channel_id=1, source_target_pairs={{0,2},{1,3},{2,0},{3,1},{4,6},{5,7},{6,4},{7,5},{8,10},{9,11},{10,... | collective-permute-start | bytes 405512 | tf_op jit(solution)/shard_map/ppermute | solution.py:35
  4.3 6.8 %collective-permute-start.4 = (bf16[528,128]{1,0:T(8,128)(2,1)S(1)}, bf16[528,128]{1,0:T(8,128)(2,1)S(1)}, u32[]{:S(2)}, u32[]{:S(2)}) collective-permute-start(bf16[528,128]{1,0:T(8,128)(2,1)S(1)} %get-tuple-element.31), channel_id=1, source_target_pairs={{0,3},{1,2},{2,1},{3,0},{4,7},{5,6},{6,5},{7,4},{8,11},{9,10},{10,... | collective-permute-start | bytes 405512 | tf_op jit(solution)/shard_map/ppermute | solution.py:35
  5.6 5.8 %collective-permute-start.1 = (bf16[2,256,128]{2,1,0:T(8,128)(2,1)S(1)}, bf16[2,256,128]{2,1,0:T(8,128)(2,1)S(1)}, u32[]{:S(2)}, u32[]{:S(2)}) collective-permute-start(bf16[2,256,128]{2,1,0:T(8,128)(2,1)S(1)} %get-tuple-element.27), channel_id=1, source_target_pairs={{0,16},{16,0},{1,17},{17,1},{2,18},{18,2},{3,19},{19,3},{4,20},{20... | collective-permute-start | bytes 393224 | tf_op jit(solution)/shard_map/ppermute | solution.py:35
  11.7 8.3 %collective-permute-start.10 = (bf16[528,128]{1,0:T(8,128)(2,1)S(1)}, bf16[528,128]{1,0:T(8,128)(2,1)S(1)}, u32[]{:S(2)}, u32[]{:S(2)}) collective-permute-start(bf16[528,128]{1,0:T(8,128)(2,1)S(1)} %get-tuple-element.41), channel_id=1, source_target_pairs={{0,12},{4,8},{8,4},{12,0},{1,13},{5,9},{9,5},{13,1},{2,14},{6,10},... | collective-permute-start | bytes 405512 | tf_op jit(solution)/shard_map/ppermute | solution.py:35
  15.6 5.3 %collective-permute-start.6 = (bf16[528,128]{1,0:T(8,128)(2,1)S(1)}, bf16[528,128]{1,0:T(8,128)(2,1)S(1)}, u32[]{:S(2)}, u32[]{:S(2)}) collective-permute-start(bf16[528,128]{1,0:T(8,128)(2,1)S(1)} %get-tuple-element.37.rest_3_), channel_id=1, source_target_pairs={{0,16},{16,0},{1,17},{17,1},{2,18},{18,2},{3,19},{19,3},{4,20},{20... | collective-permute-start | bytes 405512 | tf_op jit(solution)/shard_map/ppermute | solution.py:35
  17.1 6.4 %collective-permute-start.8 = (bf16[528,128]{1,0:T(8,128)(2,1)S(1)}, bf16[528,128]{1,0:T(8,128)(2,1)S(1)}, u32[]{:S(2)}, u32[]{:S(2)}) collective-permute-start(bf16[528,128]{1,0:T(8,128)(2,1)S(1)} %get-tuple-element.39), channel_id=1, source_target_pairs={{0,4},{4,0},{8,12},{12,8},{1,5},{5,1},{9,13},{13,9},{2,6},{6,2},{1... | collective-permute-start | bytes 405512 | tf_op jit(solution)/shard_map/ppermute | solution.py:35
  17.1 10.2 %collective-permute-start.5 = (bf16[528,128]{1,0:T(8,128)(2,1)S(1)}, bf16[528,128]{1,0:T(8,128)(2,1)S(1)}, u32[]{:S(2)}, u32[]{:S(2)}) collective-permute-start(bf16[528,128]{1,0:T(8,128)(2,1)S(1)} %get-tuple-element.36), channel_id=1, source_target_pairs={{0,8},{4,12},{8,0},{12,4},{1,9},{5,13},{9,1},{13,5},{2,10},{6,14},... | collective-permute-start | bytes 405512 | tf_op jit(solution)/shard_map/ppermute | solution.py:35
  20.9 9.2 %collective-permute-start.11 = (bf16[528,128]{1,0:T(8,128)(2,1)S(1)}, bf16[528,128]{1,0:T(8,128)(2,1)S(1)}, u32[]{:S(2)}, u32[]{:S(2)}) collective-permute-start(bf16[528,128]{1,0:T(8,128)(2,1)S(1)} %collective-permute-done.10.rest_3_), channel_id=1, source_target_pairs={{0,16},{16,0},{1,17},{17,1},{2,18},{18,2},{3,19},{19,3},{4,20},{20... | collective-permute-start | bytes 405512 | tf_op jit(solution)/shard_map/ppermute | solution.py:35
  23.5 7.0 %collective-permute-start.9 = (bf16[528,128]{1,0:T(8,128)(2,1)S(1)}, bf16[528,128]{1,0:T(8,128)(2,1)S(1)}, u32[]{:S(2)}, u32[]{:S(2)}) collective-permute-start(bf16[528,128]{1,0:T(8,128)(2,1)S(1)} %collective-permute-done.8.rest_4_), channel_id=1, source_target_pairs={{0,16},{16,0},{1,17},{17,1},{2,18},{18,2},{3,19},{19,3},{4,20},{20... | collective-permute-start | bytes 405512 | tf_op jit(solution)/shard_map/ppermute | solution.py:35
  27.3 5.0 %collective-permute-start.7 = (bf16[528,128]{1,0:T(8,128)(2,1)S(1)}, bf16[528,128]{1,0:T(8,128)(2,1)S(1)}, u32[]{:S(2)}, u32[]{:S(2)}) collective-permute-start(bf16[528,128]{1,0:T(8,128)(2,1)S(1)} %collective-permute-done.5.rest_3_), channel_id=1, source_target_pairs={{0,16},{16,0},{1,17},{17,1},{2,18},{18,2},{3,19},{19,3},{4,20},{20... | collective-permute-start | bytes 405512 | tf_op jit(solution)/shard_map/ppermute | solution.py:35
  28.8 1.3 %collective-permute-start.2 = (bf16[2,256,128]{2,1,0:T(8,128)(2,1)S(1)}, bf16[2,256,128]{2,1,0:T(8,128)(2,1)S(1)}, u32[]{:S(2)}, u32[]{:S(2)}) collective-permute-start(bf16[2,256,128]{2,1,0:T(8,128)(2,1)S(1)} %collective-permute-done.1.rest_1_), channel_id=1, source_target_pairs={{0,1},{1,0},{2,3},{3,2},{4,5},{5,4},{6,7},{7,6},{8,9},{9,8},{10,11... | collective-permute-start | bytes 393224 | tf_op jit(solution)/shard_map/ppermute | solution.py:35

commit v4 on v2

v4 whole, which is shorter than its diff:
```python
import functools

import jax
import jax.numpy as jnp
from jax import lax
from jax.experimental import pallas as pl
from jax.experimental.pallas import tpu as pltpu
from jax.sharding import PartitionSpec as P

DIGIT = 8
SLACK = 8
VMEM = pl.BlockSpec(memory_space=pltpu.VMEM)
SMEM = pl.BlockSpec(memory_space=pltpu.SMEM)
HBM = pl.BlockSpec(memory_space=pltpu.HBM)
SMALL = pltpu.CompilerParams(vmem_limit_bytes=8 * 1024 * 1024)


def mate(index, step, size):
    return index ^ step if size & (size - 1) == 0 else (index - step) % size


def target(index, step, size):
    return index ^ step if size & (size - 1) == 0 else (index + step) % size


def round_of(index, source, size):
    return index ^ source if size & (size - 1) == 0 else lax.rem(index - source + size, size)


def exchange(block, axis, step, size, stride=1):
    route = []
    for place in range(size * stride):
        high, low = divmod(place, stride)
        route.append((place, target(high, step, size) * stride + low))
    return lax.ppermute(block, axis, route)


def gated(value, after):
    return lax.optimization_barrier((value, after))[0]


def id_rows(stored):
    return -(-4 * stored // 16) * 16


def pack_kernel(stride, x_far, x2_far, *rest):
    groups, stored, side = x_far.shape[1:4]
    fars, outs, (choice, goals) = rest[:4], rest[4 : 4 + groups], rest[4 + groups : 6 + groups]
    nears, (sems, id_sems) = rest[6 + groups : 10 + groups], rest[10 + groups :]
    cols_ref, cols2_ref, wanted_ref, goals_ref = nears
    count = id_rows(stored)
    own = lax.axis_index("col")
    ids = [
        pltpu.make_async_copy(far, near, id_sems.at[at]) for at, (far, near) in enumerate(zip(fars, nears))
    ]
    loads = [
        pltpu.make_async_copy(
            (x_far, x2_far)[block // stored].at[0, target(own, step, groups), block % stored],
            out.at[pl.ds(block * side, side)],
            sems.at[step, block],
        )
        for step, out in enumerate(outs)
        for block in range(2 * stored)
    ]
    for load in ids + loads:
        load.start()
    for load in ids:
        load.wait()
    row = lax.broadcasted_iota(jnp.int32, (count, side), 0)
    for step, out in enumerate(outs):
        reader = target(own, step, groups)
        digits = jnp.zeros((count, side), jnp.int32)
        for block in range(2 * stored):
            value = (cols_ref, cols2_ref)[block // stored][0, block % stored, reader]
            digits = jnp.where(row == 2 * block, value >> DIGIT, digits)
            digits = jnp.where(row == 2 * block + 1, value & ((1 << DIGIT) - 1), digits)
        out[pl.ds(2 * stored * side, count), :] = digits.astype(jnp.float32).astype(out.dtype)
    own_row = lax.axis_index("row")
    high, low = own_row // stride, own_row % stride
    row = lax.broadcasted_iota(jnp.int32, choice.shape, 0)
    came = jnp.zeros(choice.shape, jnp.int32)
    for step in range(groups):
        reader = target(high, step, groups)
        slot = lax.rem(high - reader + groups, groups)
        owner = lax.rem(wanted_ref[0, reader * stride + low, slot], groups)
        came = jnp.where(row // groups == step, round_of(own, owner, groups), came)
    choice[...] = jnp.where(row % groups == came, 1.0, 0.0)
    row = lax.broadcasted_iota(jnp.int32, goals.shape, 0)
    goal = jnp.zeros(goals.shape, jnp.int32)
    for s in range(goals_ref.shape[2]):
        goal = jnp.where(row == s, goals_ref[0, 0, s], goal)
    goals[...] = goal.astype(jnp.float32)
    for load in loads:
        load.wait()


def pinned(array):
    return pltpu.with_memory_space_constraint(array, pltpu.HBM)


def pack(x_tiles, x2_tiles, x_cols, x2_cols, requests, out_cols, stride):
    _, groups, stored, side, _ = x_tiles.shape
    small = (jnp.swapaxes(x_cols, 1, 2), jnp.swapaxes(x2_cols, 1, 2), requests, out_cols)
    shapes = [jax.ShapeDtypeStruct((2 * stored * side + id_rows(stored), side), x_tiles.dtype)] * groups
    shapes += [
        jax.ShapeDtypeStruct((groups * groups, side), jnp.float32),
        jax.ShapeDtypeStruct((-(-out_cols.shape[2] // 8) * 8, side), jnp.float32),
    ]
    out = pl.pallas_call(
        functools.partial(pack_kernel, stride),
        out_shape=shapes,
        in_specs=[HBM] * 6,
        out_specs=[VMEM] * len(shapes),
        scratch_shapes=[pltpu.SMEM(array.shape, array.dtype) for array in small]
        + [pltpu.SemaphoreType.DMA((groups, 2 * stored)), pltpu.SemaphoreType.DMA((len(small),))],
        compiler_params=SMALL,
        name="pack",
    )(pinned(x_tiles), pinned(x2_tiles), *map(pinned, small))
    return out[:groups], out[groups], out[groups + 1]


def split_kernel(slots, slab_far, _, own_ref, *rest):
    outs, (wide, slab_ref, sems) = rest[:-3], rest[-3:]
    layers, pieces = len(outs) + 1, sems.shape[0]
    rows = slab_far.shape[0] // layers
    share = rows // pieces
    own, parity = lax.axis_index("layer"), lax.axis_index("col") % 2
    firsts = [target(own, step, layers) * rows for step in range(layers)]
    loads = [
        [
            pltpu.make_async_copy(
                slab_far.at[pl.ds(pl.multiple_of(first + at * share, share), share)],
                slab_ref.at[step, pl.ds(at * share, share)],
                sems.at[at, step],
            )
            for at in range(pieces)
        ]
        for step, first in enumerate(firsts)
    ]
    for load in sum(loads, []):
        load.start()
    for step in reversed(range(layers)):
        for load in loads[step]:
            load.wait()
        wide[pl.ds(0, rows), :] = slab_ref[step].astype(jnp.float32)
        if step:
            half = slots // 2
            for slot in range(half):
                picked = wide[pl.ds(parity * half + slot, rows // slots, stride=slots)]
                outs[step - 1][slot] = picked.astype(own_ref.dtype)
        else:
            for slot in range(slots):
                own_ref[slot] = wide[pl.ds(slot, rows // slots, stride=slots)].astype(own_ref.dtype)


def split(slab_tiles, after, layers):
    high, per, _, slots, side = slab_tiles.shape
    rows = high * per // layers
    kind = slab_tiles.dtype
    out = pl.pallas_call(
        functools.partial(split_kernel, slots),
        out_shape=[jax.ShapeDtypeStruct((slots, rows, side), kind)]
        + [jax.ShapeDtypeStruct((slots // 2, rows, side), kind)] * (layers - 1),
        in_specs=[HBM, pl.BlockSpec(memory_space=pl.ANY)],
        out_specs=[VMEM] * layers,
        scratch_shapes=[
            pltpu.VMEM((rows * slots + SLACK, side), jnp.float32),
            pltpu.VMEM((layers, rows * slots, side), kind),
            pltpu.SemaphoreType.DMA((4, layers)),
        ],
        compiler_params=SMALL,
        name="split",
    )(pinned(slab_tiles.reshape(high * per * slots, side)), after)
    return out[0], list(out[1:])


def pick_kernel(rounds, choice, *rest):
    held, outs = rest[: -len(rounds)], rest[-len(rounds) :]
    groups = len(held)
    for out, step in zip(outs, rounds):
        total = jnp.zeros(out.shape, out.dtype)
        for at in range(groups):
            place = step * groups + at
            hit = jnp.broadcast_to(choice[place : place + 1, :], out.shape).astype(out.dtype)
            total += held[at][...] * hit
        out[...] = total


def pick(choice, held, rounds):
    shape = jax.ShapeDtypeStruct(held[0].shape, held[0].dtype)
    return pl.pallas_call(
        functools.partial(pick_kernel, rounds),
        out_shape=[shape] * len(rounds),
        in_specs=[VMEM] * (1 + len(held)),
        out_specs=[VMEM] * len(rounds),
        compiler_params=SMALL,
        name="pick",
    )(choice, *held)


def product_kernel(stride, groups, items, wanted, stored, layers, last, goals, *rest):
    lefts, rest = rest[: 2 * layers - 1], list(rest[2 * layers - 1 :])
    blocks, rest = rest[: len(items)], rest[len(items) :]
    slots, rows, side = lefts[0].shape
    half = slots // 2
    high, parity = lax.axis_index("row") // stride, lax.axis_index("col") % 2
    left_parts, sums = [], ([], [])
    for (layer, step), ref in zip(items, blocks):
        slot = lax.rem(mate(high, step, groups) - high + groups, groups)
        if layer:
            same, other = lefts[2 * layer - 1], lefts[2 * layer]
            at = lax.rem(slot, half)
            left_parts.append(jnp.where(slot // half == parity, same[at], other[at]))
        else:
            left_parts.append(lefts[0][slot])
        digits = ref[pl.ds(2 * stored * side, id_rows(stored)), :].astype(jnp.float32)
        for part, chosen in enumerate(sums):
            across = [jnp.zeros((side, side), ref.dtype)] * wanted
            for block in range(part * stored, (part + 1) * stored):
                tile = ref[pl.ds(block * side, side), :]
                listed = (
                    digits[2 * block : 2 * block + 1] * (1 << DIGIT) + digits[2 * block + 1 : 2 * block + 2]
                )
                for s in range(wanted):
                    hit = jnp.where(listed == goals[s : s + 1, :], 1.0, 0.0)
                    hit = jnp.broadcast_to(hit, (side, side))
                    across[s] = across[s] + tile * hit.astype(ref.dtype)
            chosen.append(jnp.concatenate(across, axis=1))
    left = jnp.concatenate(left_parts, axis=1)
    first, second = (jnp.concatenate(chosen, axis=0) for chosen in sums)

    def term(low, high):
        return 4.0 * jnp.dot(left[low:high], first, preferred_element_type=jnp.float32) - 3.0 * jnp.dot(
            left[low:high], second, preferred_element_type=jnp.float32
        )

    if not last:
        total = term(0, rows)
        rest[-1][...] = total + rest[0][...] if len(rest) > 1 else total
        return
    total, out_far, tall, out, sems = rest
    share = rows // sems.shape[0]
    copies = []
    for at in range(sems.shape[0]):
        summed = term(at * share, (at + 1) * share) + total[pl.ds(at * share, share), :]
        part = pl.ds(at * share * wanted, share * wanted)
        for s in range(wanted):
            tall[pl.ds(at * share * wanted + s, share, stride=wanted)] = summed[:, s * side : (s + 1) * side]
        out[part] = tall[part].astype(out.dtype)
        copies.append(pltpu.make_async_copy(out.at[part], out_far.at[part], sems.at[at]))
        copies[-1].start()
    for copy in copies:
        copy.wait()


def product(lefts, blocks, total, goals, wanted, stored, stride, items, last):
    layers, groups = len(blocks), len(blocks[0])
    _, rows, side = lefts[0].shape
    flat = [blocks[layer][step] for layer, step in items] + ([] if total is None else [total])
    shape, kind = ((rows * wanted, side), lefts[0].dtype) if last else ((rows, wanted * side), jnp.float32)
    scratch = [pltpu.VMEM((shape[0] + SLACK, side), jnp.float32), pltpu.VMEM(shape, kind), pltpu.SemaphoreType.DMA((2,))]
    return pl.pallas_call(
        functools.partial(product_kernel, stride, groups, items, wanted, stored, layers, last),
        out_shape=jax.ShapeDtypeStruct(shape, kind),
        in_specs=[VMEM] * (1 + len(lefts) + len(flat)),
        out_specs=HBM if last else VMEM,
        scratch_shapes=scratch if last else [],
        compiler_params=pltpu.CompilerParams(vmem_limit_bytes=16 * 1024 * 1024),
        name="product",
    )(goals, *lefts, *flat)


def body(slab_tiles, x_tiles, x_cols, x2_tiles, x2_cols, requests, out_cols):
    layers, rows, groups = (lax.axis_size(axis) for axis in ("layer", "row", "col"))
    stride = rows // groups
    _, _, stored, side, _ = x_tiles.shape
    wanted = out_cols.shape[2]
    packed, choice, goals = pack(x_tiles, x2_tiles, x_cols, x2_cols, requests, out_cols, stride)
    held = [packed[0]] + [exchange(packed[k], "col", k, groups) for k in range(1, groups)]
    own, sent = split(slab_tiles, held[1], layers)
    sent = [exchange(sent[k - 1], "layer", k, layers) for k in range(1, layers)]
    held, sent = lax.optimization_barrier((held, sent))
    lefts = [own] + [left for same in sent for left in (same, exchange(same, "col", 1, groups))]
    picked = pick(choice, held, list(range(groups)))
    order = [*reversed(range(2, groups)), 1]
    last = order[-2]
    got = [picked[0]] + [None] * (groups - 1)
    for k in order:
        got[k] = exchange(picked[k], "row", k, groups, stride)
    blocks = [got] + [[exchange(got[0], "layer", step, layers)] + [None] * (groups - 1) for step in range(1, layers)]
    for k in order:
        block = gated(got[k], blocks[-1][0])
        for step in range(1, layers):
            blocks[step][k] = exchange(block, "layer", step, layers)

    def add(total, rounds, parts, end=False):
        items = [(layer, k) for layer in parts for k in rounds]
        return product(lefts, blocks, total, goals, wanted, stored, stride, items, end)

    everywhere = range(layers)
    total = add(None, [k for k in order if k not in (1, last)], everywhere)
    total = add(total, [0, 1], everywhere)
    total = add(total, [last], everywhere[:1])
    total = add(total, [last], everywhere[1:], True)
    high, per = slab_tiles.shape[0] // layers, slab_tiles.shape[1]
    return total.reshape(high, per, 1, wanted, side)


def solution(mesh):
    placed = (
        P(None, "row", "layer", None, None),
        P(("layer", "row", "col"), None, None, None, None),
        P(("layer", "row", "col"), None, None),
        P(("layer", "row", "col"), None, None, None, None),
        P(("layer", "row", "col"), None, None),
        P("layer", None, None),
        P("row", "col", None),
    )
    return jax.shard_map(
        body,
        mesh=mesh,
        in_specs=placed,
        out_specs=P("layer", "row", "col", None, None),
        check_vma=False,
    )
```

time: 34.5 us -> 33.6 us (0.974)
  starting transfers between devices: 18.2 us -> 15.5 us
  waiting for transfers between devices: 11.1 us -> 12.6 us
    ppermute x14 -> x12, starting transfers between devices: 18.2 us -> 15.5 us  [exchange(): return lax.ppermute(block, axis, route)]
    ppermute x14 -> x12, waiting for transfers between devices: 11.1 us -> 12.6 us  [exchange(): return lax.ppermute(block, axis, route)]
    pallas_call x5 -> x6, Pallas kernels: 3.62 us -> 3.84 us  [the longest x4 2.37 us: product(): pl.pallas_call(functools.partial(product_kernel, stride, groups, items, w...]
  transfers between devices with their start and end apart: 14 -> 12, of which waited for: 7 -> 9; matrix products, arithmetic and copies ran while one was open for 0% -> 0% of each run, Pallas kernels for 7% -> 8%
where the time goes in v4:
time: 33.6 us; the launch traced here: 33.3 us
  starting transfers between devices  15.5 us (46%)
  waiting for transfers between devices  12.6 us (38%)
  Pallas kernels  5.11 us (15%)
    ppermute x12, starting transfers between devices, exchange(): return lax.ppermute(block, axis, route)  15.5 us
    ppermute x12, waiting for transfers between devices, exchange(): return lax.ppermute(block, axis, route)  12.6 us
    pallas_call x4, Pallas kernels, product(): pl.pallas_call(functools.partial(product_kernel, stride, groups, items, w...  2.37 us
    pallas_call x1, Pallas kernels, split(): pl.pallas_call(functools.partial(split_kernel, slots), out_shape=[jax.Sha...  1.27 us
    pallas_call x1, Pallas kernels, pack(): pl.pallas_call(functools.partial(pack_kernel, stride), out_shape=shapes,...  1.17 us
  transfers between devices with their start and end apart: 12, of which 9 were waited for; matrix products, arithmetic and copies ran while one was open for 0% of the time, Pallas kernels for 8%

profile of v4, /device:TPU:0, one launch (start us, length us, event | category | flops | bytes accessed | tf_op | source)
XLA Modules:
  0.0 33.3 jit_solution(14052114882480486406)
XLA Ops:
  0.0 1.2 %pack.1 = (bf16[528,128]{1,0:T(8,128)(2,1)S(1)}, bf16[528,128]{1,0:T(8,128)(2,1)S(1)}, bf16[528,128]{1,0:T(8,128)(2,1)S(1)}, bf16[528,128]{1,0:T(8,128)(2,1)S(1)...) custom-call(bf16[1,4,2,128,128]{4,3,2,1,0:T(8,128)(2,1)} %x_far.1, bf16[1,4,2,128,128]{4,3,2,1,0:T(8,128)(2,1)} %x2_far.1, ...), custom_call_target="tpu_custom_call" | custom-call | tf_op jit(solution)/shard_map/pack/pallas_call | solution.py:109
  1.2 0.5 %collective-permute-start = (bf16[528,128]{1,0:T(8,128)(2,1)S(1)}, bf16[528,128]{1,0:T(8,128)(2,1)S(1)}, u32[]{:S(2)}, u32[]{:S(2)}) collective-permute-start(bf16[528,128]{1,0:T(8,128)(2,1)S(1)} %get-tuple-element.26), channel_id=1, source_target_pairs={{0,1},{1,0},{2,3},{3,2},{4,5},{5,4},{6,7},{7,6},{8,9},{9,8},{10,11... | collective-permute-start | bytes 405512 | tf_op jit(solution)/shard_map/ppermute | solution.py:35
  1.7 2.6 %collective-permute-start.1 = (bf16[528,128]{1,0:T(8,128)(2,1)S(1)}, bf16[528,128]{1,0:T(8,128)(2,1)S(1)}, u32[]{:S(2)}, u32[]{:S(2)}) collective-permute-start(bf16[528,128]{1,0:T(8,128)(2,1)S(1)} %get-tuple-element.29), channel_id=1, source_target_pairs={{0,2},{1,3},{2,0},{3,1},{4,6},{5,7},{6,4},{7,5},{8,10},{9,11},{10,... | collective-permute-start | bytes 405512 | tf_op jit(solution)/shard_map/ppermute | solution.py:35
  4.3 0.1 collective-permute-start.2
  4.4 0.0 collective-permute-done._.rest_1_
  4.4 1.3 %split.1 = (bf16[4,256,128]{2,1,0:T(8,128)(2,1)S(1)}, bf16[2,256,128]{2,1,0:T(8,128)(2,1)S(1)}) custom-call(bf16[2048,128]{1,0:T(8,128)(2,1)} %bitcast.6, bf16[528,128]{1,0:T(8,128)(2,1)S(1)} %collective-permute-done._.rest_1_), custom_call_target="tpu_custom_call" | custom-call | tf_op jit(solution)/shard_map/split/pallas_call | solution.py:160
  5.6 1.8 %collective-permute-start.3 = (bf16[2,256,128]{2,1,0:T(8,128)(2,1)S(1)}, bf16[2,256,128]{2,1,0:T(8,128)(2,1)S(1)}, u32[]{:S(2)}, u32[]{:S(2)}) collective-permute-start(bf16[2,256,128]{2,1,0:T(8,128)(2,1)S(1)} %get-tuple-element.31), channel_id=1, source_target_pairs={{0,16},{16,0},{1,17},{17,1},{2,18},{18,2},{3,19},{19,3},{4,20},{20... | collective-permute-start | bytes 393224 | tf_op jit(solution)/shard_map/ppermute | solution.py:35
  7.4 1.3 %collective-permute-done.1.rest_2_ = bf16[528,128]{1,0:T(8,128)(2,1)S(1)} collective-permute-done((bf16[528,128]{1,0:T(8,128)(2,1)S(1)}, bf16[528,128]{1,0:T(8,128)(2,1)S(1)}, u32[]{:S(2)}, u32[]{:S(2)}) %collective-permute-start.1) | collective-permute-done | bytes 135200 | tf_op jit(solution)/shard_map/ppermute | solution.py:35
  8.7 2.4 %collective-permute-done.2.rest_3_ = bf16[528,128]{1,0:T(8,128)(2,1)S(1)} collective-permute-done((bf16[528,128]{1,0:T(8,128)(2,1)S(1)}, bf16[528,128]{1,0:T(8,128)(2,1)S(1)}, u32[]{:S(2)}, u32[]{:S(2)}) %collective-permute-start.2) | collective-permute-done | bytes 135200 | tf_op jit(solution)/shard_map/ppermute | solution.py:35
  11.1 0.3 collective-permute-done.3.rest_1_
  11.4 0.3 pick.1
  11.7 3.9 %collective-permute-start.10 = (bf16[528,128]{1,0:T(8,128)(2,1)S(1)}, bf16[528,128]{1,0:T(8,128)(2,1)S(1)}, u32[]{:S(2)}, u32[]{:S(2)}) collective-permute-start(bf16[528,128]{1,0:T(8,128)(2,1)S(1)} %get-tuple-element.43), channel_id=1, source_target_pairs={{0,12},{4,8},{8,4},{12,0},{1,13},{5,9},{9,5},{13,1},{2,14},{6,10},... | collective-permute-start | bytes 405512 | tf_op jit(solution)/shard_map/ppermute | solution.py:35
  15.6 1.5 %collective-permute-start.6 = (bf16[528,128]{1,0:T(8,128)(2,1)S(1)}, bf16[528,128]{1,0:T(8,128)(2,1)S(1)}, u32[]{:S(2)}, u32[]{:S(2)}) collective-permute-start(bf16[528,128]{1,0:T(8,128)(2,1)S(1)} %get-tuple-element.39.rest_3_), channel_id=1, source_target_pairs={{0,16},{16,0},{1,17},{17,1},{2,18},{18,2},{3,19},{19,3},{4,20},{20... | collective-permute-start | bytes 405512 | tf_op jit(solution)/shard_map/ppermute | solution.py:35
  17.1 0.0 collective-permute-start.8
  17.1 0.8 %collective-permute-start.5 = (bf16[528,128]{1,0:T(8,128)(2,1)S(1)}, bf16[528,128]{1,0:T(8,128)(2,1)S(1)}, u32[]{:S(2)}, u32[]{:S(2)}) collective-permute-start(bf16[528,128]{1,0:T(8,128)(2,1)S(1)} %get-tuple-element.38), channel_id=1, source_target_pairs={{0,8},{4,12},{8,0},{12,4},{1,9},{5,13},{9,1},{13,5},{2,10},{6,14},... | collective-permute-start | bytes 405512 | tf_op jit(solution)/shard_map/ppermute | solution.py:35
  17.9 2.1 %collective-permute-done.10.rest_3_ = bf16[528,128]{1,0:T(8,128)(2,1)S(1)} collective-permute-done((bf16[528,128]{1,0:T(8,128)(2,1)S(1)}, bf16[528,128]{1,0:T(8,128)(2,1)S(1)}, u32[]{:S(2)}, u32[]{:S(2)}) %collective-permute-start.10) | collective-permute-done | bytes 135200 | tf_op jit(solution)/shard_map/ppermute | solution.py:35
  20.1 0.8 %collective-permute-done.6.rest_5_ = bf16[528,128]{1,0:T(8,128)(2,1)S(1)} collective-permute-done((bf16[528,128]{1,0:T(8,128)(2,1)S(1)}, bf16[528,128]{1,0:T(8,128)(2,1)S(1)}, u32[]{:S(2)}, u32[]{:S(2)}) %collective-permute-start.6) | collective-permute-done | bytes 135200 | tf_op jit(solution)/shard_map/ppermute | solution.py:35
  20.9 1.5 %collective-permute-start.11 = (bf16[528,128]{1,0:T(8,128)(2,1)S(1)}, bf16[528,128]{1,0:T(8,128)(2,1)S(1)}, u32[]{:S(2)}, u32[]{:S(2)}) collective-permute-start(bf16[528,128]{1,0:T(8,128)(2,1)S(1)} %collective-permute-done.10.rest_3_), channel_id=1, source_target_pairs={{0,16},{16,0},{1,17},{17,1},{2,18},{18,2},{3,19},{19,3},{4,20},{20... | collective-permute-start | bytes 405512 | tf_op jit(solution)/shard_map/ppermute | solution.py:35
  22.4 1.1 %collective-permute-done.8.rest_4_ = bf16[528,128]{1,0:T(8,128)(2,1)S(1)} collective-permute-done((bf16[528,128]{1,0:T(8,128)(2,1)S(1)}, bf16[528,128]{1,0:T(8,128)(2,1)S(1)}, u32[]{:S(2)}, u32[]{:S(2)}) %collective-permute-start.8) | collective-permute-done | bytes 135200 | tf_op jit(solution)/shard_map/ppermute | solution.py:35
  23.5 1.4 %collective-permute-start.9 = (bf16[528,128]{1,0:T(8,128)(2,1)S(1)}, bf16[528,128]{1,0:T(8,128)(2,1)S(1)}, u32[]{:S(2)}, u32[]{:S(2)}) collective-permute-start(bf16[528,128]{1,0:T(8,128)(2,1)S(1)} %collective-permute-done.8.rest_4_), channel_id=1, source_target_pairs={{0,16},{16,0},{1,17},{17,1},{2,18},{18,2},{3,19},{19,3},{4,20},{20... | collective-permute-start | bytes 405512 | tf_op jit(solution)/shard_map/ppermute | solution.py:35
  24.9 2.4 %collective-permute-done.5.rest_3_ = bf16[528,128]{1,0:T(8,128)(2,1)S(1)} collective-permute-done((bf16[528,128]{1,0:T(8,128)(2,1)S(1)}, bf16[528,128]{1,0:T(8,128)(2,1)S(1)}, u32[]{:S(2)}, u32[]{:S(2)}) %collective-permute-start.5) | collective-permute-done | bytes 135200 | tf_op jit(solution)/shard_map/ppermute | solution.py:35
  27.3 1.5 %collective-permute-start.7 = (bf16[528,128]{1,0:T(8,128)(2,1)S(1)}, bf16[528,128]{1,0:T(8,128)(2,1)S(1)}, u32[]{:S(2)}, u32[]{:S(2)}) collective-permute-start(bf16[528,128]{1,0:T(8,128)(2,1)S(1)} %collective-permute-done.5.rest_3_), channel_id=1, source_target_pairs={{0,16},{16,0},{1,17},{17,1},{2,18},{18,2},{3,19},{19,3},{4,20},{20... | collective-permute-start | bytes 405512 | tf_op jit(solution)/shard_map/ppermute | solution.py:35
  28.8 0.0 collective-permute-start.4
  28.8 1.3 %collective-permute-done.4.rest_2_ = bf16[2,256,128]{2,1,0:T(8,128)(2,1)S(1)} collective-permute-done((bf16[2,256,128]{2,1,0:T(8,128)(2,1)S(1)}, bf16[2,256,128]{2,1,0:T(8,128)(2,1)S(1)}, u32[]{:S(2)}, u32[]{:S(2)}) %collective-permute-start.4) | collective-permute-done | bytes 131104 | tf_op jit(solution)/shard_map/ppermute | solution.py:35
  30.1 0.0 collective-permute-done.11.rest_4_
  30.1 0.4 %product.4.rest_7_ = f32[256,512]{1,0:T(8,128)S(1)} custom-call(f32[8,128]{1,0:T(8,128)S(1)} %get-tuple-element.25.goals, bf16[4,256,128]{2,1,0:T(8,128)(2,1)S(1)} %get-tuple-element.27.rest_0_, bf16[2,256,128]{2,1,0:T(8,128)(2,1)S(1)} %collective-permute-done.3.rest_1_, bf16[2,256,128]{2,1,0:T(8,128)(2,1)S(1)} %collective-permute-done.4.rest_2_, ...), custom_call_target="tpu_custom_call" | custom-call | tf_op jit(solution)/shard_map/product/pallas_call | solution.py:262
  30.5 0.0 collective-permute-done.9.rest_6_
  30.5 0.6 %product.5.rest_4_ = f32[256,512]{1,0:T(8,128)S(1)} custom-call(f32[8,128]{1,0:T(8,128)S(1)} %get-tuple-element.25.goals, bf16[4,256,128]{2,1,0:T(8,128)(2,1)S(1)} %get-tuple-element.27.rest_0_, bf16[2,256,128]{2,1,0:T(8,128)(2,1)S(1)} %collective-permute-done.3.rest_1_, bf16[2,256,128]{2,1,0:T(8,128)(2,1)S(1)} %collective-permute-done.4.rest_2_, ...), custom_call_target="tpu_custom_call" | custom-call | tf_op jit(solution)/shard_map/product/pallas_call | solution.py:262
  31.1 0.3 %product.6.rest_4_ = f32[256,512]{1,0:T(8,128)S(1)} custom-call(f32[8,128]{1,0:T(8,128)S(1)} %get-tuple-element.25.goals, bf16[4,256,128]{2,1,0:T(8,128)(2,1)S(1)} %get-tuple-element.27.rest_0_, bf16[2,256,128]{2,1,0:T(8,128)(2,1)S(1)} %collective-permute-done.3.rest_1_, bf16[2,256,128]{2,1,0:T(8,128)(2,1)S(1)} %collective-permute-done.4.rest_2_, ...), custom_call_target="tpu_custom_call" | custom-call | tf_op jit(solution)/shard_map/product/pallas_call | solution.py:262
  31.5 0.8 %collective-permute-done.7.rest_3_ = bf16[528,128]{1,0:T(8,128)(2,1)S(1)} collective-permute-done((bf16[528,128]{1,0:T(8,128)(2,1)S(1)}, bf16[528,128]{1,0:T(8,128)(2,1)S(1)}, u32[]{:S(2)}, u32[]{:S(2)}) %collective-permute-start.7) | collective-permute-done | bytes 135200 | tf_op jit(solution)/shard_map/ppermute | solution.py:35
  32.3 1.0 %product.7 = bf16[1024,128]{1,0:T(8,128)(2,1)} custom-call(f32[8,128]{1,0:T(8,128)S(1)} %get-tuple-element.25.goals, bf16[4,256,128]{2,1,0:T(8,128)(2,1)S(1)} %get-tuple-element.27.rest_0_, bf16[2,256,128]{2,1,0:T(8,128)(2,1)S(1)} %collective-permute-done.3.rest_1_, bf16[2,256,128]{2,1,0:T(8,128)(2,1)S(1)} %collective-permute-done.4.rest_2_, ...), custom_call_target="tpu_custom_call" | custom-call | tf_op jit(solution)/shard_map/product/pallas_call | solution.py:262
Async XLA Ops:
  1.2 3.2 %collective-permute-start = (bf16[528,128]{1,0:T(8,128)(2,1)S(1)}, bf16[528,128]{1,0:T(8,128)(2,1)S(1)}, u32[]{:S(2)}, u32[]{:S(2)}) collective-permute-start(bf16[528,128]{1,0:T(8,128)(2,1)S(1)} %get-tuple-element.26), channel_id=1, source_target_pairs={{0,1},{1,0},{2,3},{3,2},{4,5},{5,4},{6,7},{7,6},{8,9},{9,8},{10,11... | collective-permute-start | bytes 405512 | tf_op jit(solution)/shard_map/ppermute | solution.py:35
  1.7 7.0 %collective-permute-start.1 = (bf16[528,128]{1,0:T(8,128)(2,1)S(1)}, bf16[528,128]{1,0:T(8,128)(2,1)S(1)}, u32[]{:S(2)}, u32[]{:S(2)}) collective-permute-start(bf16[528,128]{1,0:T(8,128)(2,1)S(1)} %get-tuple-element.29), channel_id=1, source_target_pairs={{0,2},{1,3},{2,0},{3,1},{4,6},{5,7},{6,4},{7,5},{8,10},{9,11},{10,... | collective-permute-start | bytes 405512 | tf_op jit(solution)/shard_map/ppermute | solution.py:35
  4.3 6.8 %collective-permute-start.2 = (bf16[528,128]{1,0:T(8,128)(2,1)S(1)}, bf16[528,128]{1,0:T(8,128)(2,1)S(1)}, u32[]{:S(2)}, u32[]{:S(2)}) collective-permute-start(bf16[528,128]{1,0:T(8,128)(2,1)S(1)} %get-tuple-element.30), channel_id=1, source_target_pairs={{0,3},{1,2},{2,1},{3,0},{4,7},{5,6},{6,5},{7,4},{8,11},{9,10},{10,... | collective-permute-start | bytes 405512 | tf_op jit(solution)/shard_map/ppermute | solution.py:35
  5.6 5.8 %collective-permute-start.3 = (bf16[2,256,128]{2,1,0:T(8,128)(2,1)S(1)}, bf16[2,256,128]{2,1,0:T(8,128)(2,1)S(1)}, u32[]{:S(2)}, u32[]{:S(2)}) collective-permute-start(bf16[2,256,128]{2,1,0:T(8,128)(2,1)S(1)} %get-tuple-element.31), channel_id=1, source_target_pairs={{0,16},{16,0},{1,17},{17,1},{2,18},{18,2},{3,19},{19,3},{4,20},{20... | collective-permute-start | bytes 393224 | tf_op jit(solution)/shard_map/ppermute | solution.py:35
  11.7 8.3 %collective-permute-start.10 = (bf16[528,128]{1,0:T(8,128)(2,1)S(1)}, bf16[528,128]{1,0:T(8,128)(2,1)S(1)}, u32[]{:S(2)}, u32[]{:S(2)}) collective-permute-start(bf16[528,128]{1,0:T(8,128)(2,1)S(1)} %get-tuple-element.43), channel_id=1, source_target_pairs={{0,12},{4,8},{8,4},{12,0},{1,13},{5,9},{9,5},{13,1},{2,14},{6,10},... | collective-permute-start | bytes 405512 | tf_op jit(solution)/shard_map/ppermute | solution.py:35
  15.6 5.3 %collective-permute-start.6 = (bf16[528,128]{1,0:T(8,128)(2,1)S(1)}, bf16[528,128]{1,0:T(8,128)(2,1)S(1)}, u32[]{:S(2)}, u32[]{:S(2)}) collective-permute-start(bf16[528,128]{1,0:T(8,128)(2,1)S(1)} %get-tuple-element.39.rest_3_), channel_id=1, source_target_pairs={{0,16},{16,0},{1,17},{17,1},{2,18},{18,2},{3,19},{19,3},{4,20},{20... | collective-permute-start | bytes 405512 | tf_op jit(solution)/shard_map/ppermute | solution.py:35
  17.1 6.4 %collective-permute-start.8 = (bf16[528,128]{1,0:T(8,128)(2,1)S(1)}, bf16[528,128]{1,0:T(8,128)(2,1)S(1)}, u32[]{:S(2)}, u32[]{:S(2)}) collective-permute-start(bf16[528,128]{1,0:T(8,128)(2,1)S(1)} %get-tuple-element.41), channel_id=1, source_target_pairs={{0,4},{4,0},{8,12},{12,8},{1,5},{5,1},{9,13},{13,9},{2,6},{6,2},{1... | collective-permute-start | bytes 405512 | tf_op jit(solution)/shard_map/ppermute | solution.py:35
  17.1 10.2 %collective-permute-start.5 = (bf16[528,128]{1,0:T(8,128)(2,1)S(1)}, bf16[528,128]{1,0:T(8,128)(2,1)S(1)}, u32[]{:S(2)}, u32[]{:S(2)}) collective-permute-start(bf16[528,128]{1,0:T(8,128)(2,1)S(1)} %get-tuple-element.38), channel_id=1, source_target_pairs={{0,8},{4,12},{8,0},{12,4},{1,9},{5,13},{9,1},{13,5},{2,10},{6,14},... | collective-permute-start | bytes 405512 | tf_op jit(solution)/shard_map/ppermute | solution.py:35
  20.9 9.2 %collective-permute-start.11 = (bf16[528,128]{1,0:T(8,128)(2,1)S(1)}, bf16[528,128]{1,0:T(8,128)(2,1)S(1)}, u32[]{:S(2)}, u32[]{:S(2)}) collective-permute-start(bf16[528,128]{1,0:T(8,128)(2,1)S(1)} %collective-permute-done.10.rest_3_), channel_id=1, source_target_pairs={{0,16},{16,0},{1,17},{17,1},{2,18},{18,2},{3,19},{19,3},{4,20},{20... | collective-permute-start | bytes 405512 | tf_op jit(solution)/shard_map/ppermute | solution.py:35
  23.5 7.0 %collective-permute-start.9 = (bf16[528,128]{1,0:T(8,128)(2,1)S(1)}, bf16[528,128]{1,0:T(8,128)(2,1)S(1)}, u32[]{:S(2)}, u32[]{:S(2)}) collective-permute-start(bf16[528,128]{1,0:T(8,128)(2,1)S(1)} %collective-permute-done.8.rest_4_), channel_id=1, source_target_pairs={{0,16},{16,0},{1,17},{17,1},{2,18},{18,2},{3,19},{19,3},{4,20},{20... | collective-permute-start | bytes 405512 | tf_op jit(solution)/shard_map/ppermute | solution.py:35
  27.3 5.0 %collective-permute-start.7 = (bf16[528,128]{1,0:T(8,128)(2,1)S(1)}, bf16[528,128]{1,0:T(8,128)(2,1)S(1)}, u32[]{:S(2)}, u32[]{:S(2)}) collective-permute-start(bf16[528,128]{1,0:T(8,128)(2,1)S(1)} %collective-permute-done.5.rest_3_), channel_id=1, source_target_pairs={{0,16},{16,0},{1,17},{17,1},{2,18},{18,2},{3,19},{19,3},{4,20},{20... | collective-permute-start | bytes 405512 | tf_op jit(solution)/shard_map/ppermute | solution.py:35
  28.8 1.3 %collective-permute-start.4 = (bf16[2,256,128]{2,1,0:T(8,128)(2,1)S(1)}, bf16[2,256,128]{2,1,0:T(8,128)(2,1)S(1)}, u32[]{:S(2)}, u32[]{:S(2)}) collective-permute-start(bf16[2,256,128]{2,1,0:T(8,128)(2,1)S(1)} %collective-permute-done.3.rest_1_), channel_id=1, source_target_pairs={{0,1},{1,0},{2,3},{3,2},{4,5},{5,4},{6,7},{7,6},{8,9},{9,8},{10,11... | collective-permute-start | bytes 393224 | tf_op jit(solution)/shard_map/ppermute | solution.py:35
